TPU v7x, 32 devices: a whole 2x2x4 slice. The times are simulated.
32 devices in a mesh: risk: 16 (over z, y, x), tcol: 2 (over core).
Axes of the slice: x: 2, y: 2, z: 4, core: 2. Of those that a mesh axis runs over, the one named last changes fastest.
Arguments:
- idio_normals: bfloat16 [128, 131072], P('tcol', 'risk'), may hold values from -6 to 6
- factor_normals: bfloat16 [128, 64], P('tcol'), may hold values from -6 to 6
- loadings: bfloat16 [64, 131072], P(None, 'risk'), may hold values from -0.75 to 0.75
- log_scale: float32 [131072], P('risk'), may hold values from -1.5 to 0
- sigma: float32 [131072], P('risk'), may hold values from 0.2 to 0.7
- idio_weight: float32 [131072], P('risk'), may hold values from 0.3 to 1
- risk_slot: int32 [131072], P('risk'), may hold values from 0 to 127
- tile_owner: int32 [1024, 1], P('risk'), may hold values from 0 to 15; in each aligned block of 64 rows (0 to 63, 64 to 127, ...) at most 8 rows name the same one
- tile_sub: int32 [1024], P('risk'), may hold values from 0 to 5
- attach: float32 [12288], P('risk'), may hold values from 2 to 16
- limit: float32 [12288], P('risk'), may hold values from 2 to 20
- share_values: bfloat16 [96, 2, 128, 128], P('risk', None, 'tcol'), may hold values from 0 to 0.0012969971
- share_rblock: int32 [96, 2], P('risk'), may hold values from 0 to 3, all different within a row
Outputs:
- ceded_loss: float32 [128, 12288], P('tcol', 'risk')
- reinsurer_loss: float32 [128, 512], P('tcol', 'risk')
Inputs may be any that keep to these rules, and one draw needn't show every extreme that they name: `tile_owner`: among the 64 tiles of one index of risk no owner is named more than 8 times, a bound that some block reaches. `share_rblock`: the 2 tiles of one treaty block name distinct reinsurer blocks.
All inputs are finite; a program needn't handle non-finite values.
Results may differ from a plain program's by a relative error of at most 0.0019.
Values may be sent and summed in bfloat16 or wider, within the bound.
No kernel may reach another device: no remote copies, remote signals or barrier semaphores. Data moves between devices by JAX's collectives and lax.ppermute only.
A program may use at most 64 MiB of HBM per device.

v0:
```python
import jax
import jax.numpy as jnp
from jax import lax
from jax.sharding import PartitionSpec as P

TB = 128
RB = 128
REINS = 512


def on_device(
    idio_normals,
    factor_normals,
    loadings,
    log_scale,
    sigma,
    idio_weight,
    risk_slot,
    tile_owner,
    tile_sub,
    attach,
    limit,
    share_values,
    share_rblock,
):
    risk_count = lax.axis_size("risk")
    years_dev, risk_dev = idio_normals.shape
    tile_count = tile_sub.shape[0]
    tile_rows = risk_dev // tile_count
    blocks_owned = attach.shape[0] // TB
    common = jnp.dot(factor_normals, loadings, preferred_element_type=jnp.float32)
    latent = common + idio_weight * idio_normals.astype(jnp.float32)
    losses = jnp.exp(log_scale + sigma * latent).astype(jnp.bfloat16)
    onehot = (
        risk_slot.reshape(tile_count, tile_rows)[:, :, None]
        == jnp.arange(TB, dtype=jnp.int32)[None, None, :]
    ).astype(jnp.bfloat16)
    partials = jnp.einsum(
        "ykr,krb->kyb",
        losses.reshape(years_dev, tile_count, tile_rows),
        onehot,
        preferred_element_type=jnp.float32,
    )
    owners = tile_owner[:, 0]
    capacity = 2 * tile_count // risk_count
    matches = owners[:, None] == owners[None, :]
    earlier = jnp.arange(tile_count)[None, :] < jnp.arange(tile_count)[:, None]
    position = jnp.sum(jnp.logical_and(matches, earlier), axis=1)
    slot_id = owners * capacity + position
    outbound = (
        jnp.zeros((risk_count * capacity, years_dev, TB), jnp.float32).at[slot_id].set(partials)
    )
    outbound = outbound.reshape(risk_count, capacity, years_dev, TB)
    sub_ids = (
        jnp.zeros((risk_count * capacity,), jnp.float32)
        .at[slot_id]
        .set(tile_sub.astype(jnp.float32))
    )
    sub_ids = sub_ids.reshape(risk_count, capacity)
    inbound, inbound_ids = (
        lax.all_to_all(outbound, "risk", split_axis=0, concat_axis=0, tiled=True),
        lax.all_to_all(sub_ids, "risk", split_axis=0, concat_axis=0, tiled=True),
    )
    selector = (
        inbound_ids.reshape(-1)[:, None] == jnp.arange(blocks_owned, dtype=jnp.float32)[None, :]
    ).astype(jnp.float32)
    gross = jnp.einsum(
        "sg,syb->ygb", selector, inbound.reshape(-1, years_dev, TB), precision=lax.Precision.HIGHEST
    )
    ceded = jnp.minimum(
        jnp.maximum(gross - attach.reshape(1, blocks_owned, TB), 0.0),
        limit.reshape(1, blocks_owned, TB),
    )
    ceded_low = ceded.astype(jnp.bfloat16)
    rein_blocks = REINS // RB
    selector_low = (
        share_rblock[:, :, None] == jnp.arange(rein_blocks, dtype=jnp.int32)[None, None, :]
    ).astype(jnp.bfloat16)
    shares = lax.all_gather(share_values, "tcol", axis=2, tiled=True)
    count_rows = shares.shape[2]
    spread = jnp.einsum("gkr,gktj->gtrj", selector_low, shares, preferred_element_type=jnp.float32)
    spread = spread.astype(jnp.bfloat16).reshape(blocks_owned, count_rows, REINS)
    retro_terms = jnp.einsum("ygt,gtr->yr", ceded_low, spread, preferred_element_type=jnp.float32)
    reinsurer_loss = lax.psum_scatter(retro_terms, "risk", scatter_dimension=1, tiled=True)
    return (ceded.reshape(years_dev, blocks_owned * TB), reinsurer_loss)


def solution(mesh):
    placed = (
        P("tcol", "risk"),
        P("tcol", None),
        P(None, "risk"),
        P("risk"),
        P("risk"),
        P("risk"),
        P("risk"),
        P("risk", None),
        P("risk"),
        P("risk"),
        P("risk"),
        P("risk", None, "tcol", None),
        P("risk", None),
    )
    return jax.shard_map(
        on_device,
        mesh=mesh,
        in_specs=placed,
        out_specs=(P("tcol", "risk"), P("tcol", "risk")),
        check_vma=False,
    )
```

profile of v0, /device:TPU:0, one launch (start us, length us, event | category | flops | bytes accessed | tf_op | source)
XLA Modules:
  0.0 230.1 jit_solution(8299921050390908947)
XLA Ops:
  7.2 0.0 copy-start
  7.2 0.0 copy-start.2
  7.2 0.9 convert_reduce_fusion
  8.1 0.7 fusion.34
  8.8 0.7 convert_element_type.27
  9.5 0.8 scatter_custom_fusion.1
  10.2 0.7 all_to_all.10
  10.9 8.3 %all-to-all-start.1 = ((f32[16,1,8]{2,1,0:T(1,128)}), f32[16,1,8]{2,1,0:T(1,128)S(1)}, u32[]{:S(2)}, u32[]{:S(2)}) async-start(f32[16,1,8]{2,1,0:T(1,128)} %bitcast.6), calls=%async_computation.1 | async-start | bytes 16384 | tf_op jit(solution)/shard_map/all_to_all | solution.py:62
  19.2 0.0 copy-done
  19.3 2.0 fusion.9
  21.3 0.0 copy-done.2
  21.3 2.9 %fusion.7 = f32[64,64,128]{2,1,0:T(8,128)S(1)} fusion(s32[64,128]{1,0:T(8,128)S(1)} %bitcast.65, bf16[8,64,8,128]{3,2,1,0:T(8,128)(2,1)S(1)} %fusion.9), kind=kOutput, calls=%fused_computation.11 | convolution fusion | flops 135266304 | bytes 3178496 | tf_op jit(solution)/shard_map/ykr,krb->kyb/dot_general | solution.py:38
  24.1 2.5 %broadcast_in_dim.4 = f32[128,64,128]{2,1,0:T(8,128)} broadcast(f32[]{:T(128)} %constant.4.clone.1), dimensions={} | broadcast | bytes 4194308 | tf_op jit(solution)/shard_map/broadcast_in_dim | solution.py:51
  26.6 8.6 %scatter_fusion = f32[128,64,128]{2,1,0:T(8,128)} fusion(f32[128,64,128]{2,1,0:T(8,128)} %broadcast_in_dim.4, s32[64]{0:T(128)S(1)} %fusion.34, f32[64,64,128]{2,1,0:T(8,128)S(1)} %fusion.7), kind=kCustom, calls=%fused_computation | custom fusion | bytes 6291712 | tf_op jit(solution)/shard_map/scatter | solution.py:51
  35.2 7.4 %copy.35 = f32[16,8,64,128]{3,1,2,0:T(8,128)} copy(f32[16,8,64,128]{3,2,1,0:T(8,128)} %bitcast.61) | data formatting | bytes 8388608 | tf_op jit(solution)/shard_map/reshape | solution.py:53
  42.6 0.0 copy-start.1
  42.7 0.0 copy-start.5
  42.7 0.0 all-to-all-done.1
  42.7 7.1 %all-to-all-start = ((f32[16,8,64,128]{3,1,2,0:T(8,128)}), f32[16,8,64,128]{3,1,2,0:T(8,128)}, u32[]{:S(2)}, u32[]{:S(2)}) async-start(f32[16,8,64,128]{3,1,2,0:T(8,128)} %copy.35), calls=%async_computation | async-start | bytes 8388608 | tf_op jit(solution)/shard_map/all_to_all | solution.py:61
  49.7 0.0 copy-start.3
  49.7 0.0 copy-start.4
  49.7 0.0 reduce-scatter.2.cloned.1.call-start
  49.8 0.0 copy-done.1
  49.8 0.2 copy.39
  50.0 0.0 copy-done.5
  50.0 0.1 copy.38
  50.1 2.1 all_gather.3
  52.2 0.8 fusion.10
  53.0 0.6 copy.44
  53.5 0.5 broadcast.20
  54.0 0.7 reduce.3
  54.7 0.1 eq.66
  54.8 73.6 %all-to-all-done = f32[16,8,64,128]{3,1,2,0:T(8,128)} async-done(((f32[16,8,64,128]{3,1,2,0:T(8,128)}), f32[16,8,64,128]{3,1,2,0:T(8,128)}, u32[]{:S(2)}, u32[]{:S(2)}) %all-to-all-start) | async-done | bytes 4194336 | tf_op jit(solution)/shard_map/all_to_all | solution.py:61
  128.4 0.0 copy-done.3
  128.4 0.0 copy-done.4
  128.4 3.6 %fusion.37 = (bf16[64,6,128]{2,1,0:T(8,128)(2,1)S(1)}, f32[64,6,128]{2,1,0:T(8,128)S(1)}) fusion(f32[6,128]{1,0:T(8,128)S(1)} %bitcast.66, f32[6,128]{1,0:T(8,128)S(1)} %bitcast.67, f32[128]{0:T(128)S(1)} %eq.66, f32[16,8,64,128]{3,1,2,0:T(8,128)} %all-to-all-done), kind=kOutput, calls=%fused_computation.40 | convolution fusion | flops 75694848 | bytes 4495872 | tf_op jit(solution)/shard_map/sg,syb->ygb/dot_general | solution.py:67
  132.1 1.0 convolution_bitcast_fusion
  133.1 0.0 reduce-scatter.2.cloned.1.call-update
  133.1 0.7 copy.68
  133.8 89.4 %reduce-scatter.2.cloned.1.call-done = f32[64,32]{0,1:T(8,128)} async-done(((f32[64,512]{0,1:T(8,128)}), f32[64,32]{0,1:T(8,128)}) %reduce-scatter.2.cloned.1.call-update) | async-done | bytes 8208 | tf_op jit(solution)/shard_map/reduce_scatter | solution.py:84
Async XLA Ops:
  7.2 12.1 %copy-start = (bf16[64,8192]{1,0:T(8,128)(2,1)S(1)}, bf16[64,8192]{1,0:T(8,128)(2,1)}, u32[]{:S(2)}) copy-start(bf16[64,8192]{1,0:T(8,128)(2,1)} %param.15) | copy-start | bytes 3145732
  7.2 14.1 %copy-start.2 = (s32[8192]{0:T(1024)S(1)}, s32[8192]{0:T(1024)}, u32[]{:S(2)}) copy-start(s32[8192]{0:T(1024)} %param.19) | copy-start | bytes 98308
  10.9 31.7 %all-to-all-start.1 = ((f32[16,1,8]{2,1,0:T(1,128)}), f32[16,1,8]{2,1,0:T(1,128)S(1)}, u32[]{:S(2)}, u32[]{:S(2)}) async-start(f32[16,1,8]{2,1,0:T(1,128)} %bitcast.6), calls=%async_computation.1 | async-start | bytes 16384 | tf_op jit(solution)/shard_map/all_to_all | solution.py:62
  42.6 7.2 %copy-start.1 = (bf16[6,2,64,128]{3,2,1,0:T(8,128)(2,1)S(1)}, bf16[6,2,64,128]{3,2,1,0:T(8,128)(2,1)}, u32[]{:S(2)}) copy-start(bf16[6,2,64,128]{3,2,1,0:T(8,128)(2,1)} %param.24) | copy-start | bytes 589828
  42.7 7.4 %copy-start.5 = (s32[6,2]{0,1:T(2,128)S(1)}, s32[6,2]{0,1:T(2,128)}, u32[]{:S(2)}) copy-start(s32[6,2]{0,1:T(2,128)} %param.25) | copy-start | bytes 148
  42.7 85.8 %all-to-all-start = ((f32[16,8,64,128]{3,1,2,0:T(8,128)}), f32[16,8,64,128]{3,1,2,0:T(8,128)}, u32[]{:S(2)}, u32[]{:S(2)}) async-start(f32[16,8,64,128]{3,1,2,0:T(8,128)} %copy.35), calls=%async_computation | async-start | bytes 8388608 | tf_op jit(solution)/shard_map/all_to_all | solution.py:61
  49.7 78.7 %copy-start.3 = (f32[768]{0:T(1024)S(1)}, f32[768]{0:T(1024)}, u32[]{:S(2)}) copy-start(f32[768]{0:T(1024)} %param.23) | copy-start | bytes 9220
  49.7 78.7 %copy-start.4 = (f32[768]{0:T(1024)S(1)}, f32[768]{0:T(1024)}, u32[]{:S(2)}) copy-start(f32[768]{0:T(1024)} %param.22) | copy-start | bytes 9220
  49.7 173.5 %reduce-scatter.2.cloned.1.call-start = ((), (), s32[]{:S(2)}) async-start(), calls=%async_computation.3 | async-start | bytes 278528 | tf_op jit(solution)/shard_map/reduce_scatter | solution.py:84
Sparse Core Ops, SparseCore 0:
  133.2 89.9 reduce-scatter.1
where the time goes:
time: 231 us; the launch traced here: 230 us
  waiting for transfers between devices  163 us (71%)
  local copies, waits for them, and re-layouts  22.2 us (10%)
  starting transfers between devices  15.4 us (7%)
  between operations  14.2 us (6%)
  matrix products  10.3 us (4%)
  other arithmetic  2.93 us (1%)
    reduce_scatter x1, waiting for transfers between devices, on_device(): lax.psum_scatter(retro_terms, 'risk', scatter_dimension=1, tiled=True)  89.4 us
    all_to_all x1, waiting for transfers between devices, on_device(): lax.all_to_all(outbound, 'risk', split_axis=0, concat_axis=0, tiled=True)  73.6 us
    scatter x1, local copies, waits for them, and re-layouts, on_device(): jnp.zeros((risk_count * capacity, years_dev, TB), jnp.float32).at[slot_id]  8.61 us
    all_to_all x1, starting transfers between devices, on_device(): lax.all_to_all(sub_ids, 'risk', split_axis=0, concat_axis=0, tiled=True)  8.31 us
    reshape x1, local copies, waits for them, and re-layouts, on_device(): outbound = outbound.reshape(risk_count, capacity, years_dev, TB)  7.4 us
    all_to_all x1, starting transfers between devices, on_device(): lax.all_to_all(outbound, 'risk', split_axis=0, concat_axis=0, tiled=True)  7.06 us
  transfers between devices with their start and end apart: 3, of which 2 were waited for; matrix products, arithmetic and copies ran while one was open for 12% of the time, Pallas kernels for 0%

commit v1 on v0

--- a/solution.py
+++ b/solution.py
@@ -1,27 +1,178 @@
 import jax
 import jax.numpy as jnp
 from jax import lax
+from jax.experimental import pallas as pl
+from jax.experimental.pallas import tpu as pltpu
 from jax.sharding import PartitionSpec as P
 
 TB = 128
 RB = 128
 REINS = 512
-
-
-def on_device(
-    idio_normals,
-    factor_normals,
-    loadings,
-    log_scale,
-    sigma,
-    idio_weight,
-    risk_slot,
-    tile_owner,
-    tile_sub,
-    attach,
-    limit,
-    share_values,
-    share_rblock,
+TOP = 40.0
+SCALE = 65535.0 / TOP
+HALF = 32768
+
+
+def encode(sums):
+    steps = jnp.minimum(sums * SCALE + 0.5, 65535.0).astype(jnp.int32) - HALF
+    return steps.astype(jnp.int16)
+
+
+def decode(coded):
+    return (coded.astype(jnp.int32) + HALF).astype(jnp.float32) * (1.0 / SCALE)
+
+
+def block_sums_kernel(
+    owner_ref, sub_ref, idio_ref, factor_ref, loads_ref, scale_ref, sigma_ref, weight_ref, slot_ref,
+    out_ref, acc_ref,
+):
+    blocks_owned = acc_ref.shape[0] // lax.axis_size("risk")
+    step = pl.program_id(0)
+    tiles = scale_ref.shape[0]
+
+    @pl.when(step == 0)
+    def _():
+        acc_ref[...] = jnp.zeros_like(acc_ref)
+
+    factor = factor_ref[...]
+    rows = lax.broadcasted_iota(jnp.int32, (TB, TB), 0)
+    for k in range(tiles):
+        cols = pl.ds(k * TB, TB)
+        common = jnp.dot(factor, loads_ref[:, cols], preferred_element_type=jnp.float32)
+        latent = common + weight_ref[pl.ds(k, 1), :] * idio_ref[:, cols].astype(jnp.float32)
+        losses = jnp.exp(scale_ref[pl.ds(k, 1), :] + sigma_ref[pl.ds(k, 1), :] * latent)
+        chosen = (rows == slot_ref[pl.ds(k, 1), :]).astype(jnp.float32).astype(jnp.bfloat16)
+        sums = lax.dot_general(
+            losses.astype(jnp.bfloat16), chosen, (((1,), (1,)), ((), ())),
+            preferred_element_type=jnp.float32,
+        )
+        tile = step * tiles + k
+        at = owner_ref[tile] * blocks_owned + sub_ref[tile]
+        acc_ref[at] += sums
+
+    @pl.when(step == pl.num_programs(0) - 1)
+    def _():
+        def body(b, carry):
+            out_ref[b] = encode(acc_ref[b])
+            return carry
+
+        lax.fori_loop(0, acc_ref.shape[0], body, 0, unroll=4)
+
+
+def block_sums(idio, factor, loads, log_scale, sigma, weight, slot, owner, sub, blocks, steps=4):
+    years, risks = idio.shape
+    tiles = sub.shape[0]
+    per = tiles // steps
+    fold = lambda a: a.reshape(tiles, TB)
+    row = pl.BlockSpec((per, TB), lambda i: (i, 0))
+    smem = pl.BlockSpec(memory_space=pltpu.SMEM)
+    return pl.pallas_call(
+        block_sums_kernel,
+        grid=(steps,),
+        in_specs=[
+            smem,
+            smem,
+            pl.BlockSpec((years, per * TB), lambda i: (0, i)),
+            pl.BlockSpec(factor.shape, lambda i: (0, 0)),
+            pl.BlockSpec((loads.shape[0], per * TB), lambda i: (0, i)),
+            row,
+            row,
+            row,
+            row,
+        ],
+        out_specs=pl.BlockSpec((blocks, years, TB), lambda i: (0, 0, 0)),
+        out_shape=jax.ShapeDtypeStruct((blocks, years, TB), jnp.int16),
+        scratch_shapes=[pltpu.VMEM((blocks, years, TB), jnp.float32)],
+        compiler_params=pltpu.CompilerParams(vmem_limit_bytes=40 * 2**20),
+    )(owner.reshape(-1), sub, idio, factor, loads, fold(log_scale), fold(sigma), fold(weight), fold(slot))
+
+
+def retro_kernel(rblock_ref, inbound_ref, attach_ref, limit_ref, mine_ref, other_ref, ceded_ref, out_ref, acc_ref):
+    sources, owned, years, _ = inbound_ref.shape
+    tiles = mine_ref.shape[1]
+    first = lax.axis_index("tcol") == 0
+    acc_ref[...] = jnp.zeros_like(acc_ref)
+    for g in range(owned):
+        gross = decode(inbound_ref[0, g])
+        for s in range(1, sources):
+            gross += decode(inbound_ref[s, g])
+        ceded = jnp.minimum(jnp.maximum(gross - attach_ref[pl.ds(g, 1), :], 0.0), limit_ref[pl.ds(g, 1), :])
+        ceded_ref[:, pl.ds(g * TB, TB)] = ceded
+        low = ceded.astype(jnp.bfloat16)
+        for k in range(tiles):
+            mine, other = mine_ref[g, k], other_ref[g, k]
+            top = jnp.where(first, mine, other)
+            bottom = jnp.where(first, other, mine)
+            part = jnp.dot(low, jnp.concatenate([top, bottom], axis=0), preferred_element_type=jnp.float32)
+            acc_ref[rblock_ref[g, k]] += part
+    wide = RB // 4
+    quarter = years // 4
+    lane = lax.broadcasted_iota(jnp.int32, (quarter, RB), 1) // wide
+    for q in range(acc_ref.shape[0]):
+        parts = [acc_ref[q, pl.ds(j * quarter, quarter), :] for j in range(4)]
+        for i in range(4):
+            packed = parts[i]
+            for j in range(4):
+                if j != i:
+                    moved = pltpu.roll(parts[j], ((j - i) * wide) % RB, 1)
+                    packed = jnp.where(lane == j, moved, packed)
+            out_ref[4 * q + i] = packed
+
+
+def retro(inbound, attach, limit, mine, other, rblock):
+    sources, owned, years, _ = inbound.shape
+    vmem = pl.BlockSpec(memory_space=pltpu.VMEM)
+    return pl.pallas_call(
+        retro_kernel,
+        in_specs=[pl.BlockSpec(memory_space=pltpu.SMEM)] + [vmem] * 5,
+        out_specs=[vmem, vmem],
+        out_shape=[
+            jax.ShapeDtypeStruct((years, owned * TB), jnp.float32),
+            jax.ShapeDtypeStruct((REINS * 4 // RB, years // 4, RB), jnp.float32),
+        ],
+        scratch_shapes=[pltpu.VMEM((REINS // RB, years, RB), jnp.float32)],
+        compiler_params=pltpu.CompilerParams(vmem_limit_bytes=40 * 2**20),
+    )(rblock, inbound, attach.reshape(owned, TB), limit.reshape(owned, TB), mine, other)
+
+
+def finish_kernel(in_ref, out_ref):
+    total = in_ref[0]
+    for s in range(1, in_ref.shape[0]):
+        total += in_ref[s]
+    quarter, wide = total.shape[0], RB // 4
+    for j in range(4):
+        out_ref[pl.ds(j * quarter, quarter), :] = total[:, j * wide : (j + 1) * wide]
+
+
+def finish(pieces):
+    return pl.pallas_call(
+        finish_kernel,
+        out_shape=jax.ShapeDtypeStruct((pieces.shape[1] * 4, RB // 4), jnp.float32),
+    )(pieces)
+
+
+def dense_on_device(
+    idio_normals, factor_normals, loadings, log_scale, sigma, idio_weight, risk_slot,
+    tile_owner, tile_sub, attach, limit, share_values, share_rblock,
+):
+    risk_count = lax.axis_size("risk")
+    years_dev = idio_normals.shape[0]
+    owned = attach.shape[0] // TB
+    other_shares = lax.ppermute(share_values, "tcol", [(0, 1), (1, 0)])
+    outbound = block_sums(
+        idio_normals, factor_normals, loadings, log_scale, sigma, idio_weight, risk_slot,
+        tile_owner, tile_sub, risk_count * owned,
+    )
+    inbound = lax.all_to_all(outbound, "risk", split_axis=0, concat_axis=0, tiled=True)
+    inbound = inbound.reshape(risk_count, owned, years_dev, TB)
+    ceded, pieces = retro(inbound, attach, limit, share_values, other_shares, share_rblock)
+    pieces = lax.all_to_all(pieces, "risk", split_axis=0, concat_axis=0, tiled=True)
+    return ceded, finish(pieces)
+
+
+def sparse_on_device(
+    idio_normals, factor_normals, loadings, log_scale, sigma, idio_weight, risk_slot,
+    tile_owner, tile_sub, attach, limit, share_values, share_rblock,
 ):
     risk_count = lax.axis_size("risk")
     years_dev, risk_dev = idio_normals.shape
@@ -101,8 +252,9 @@
         P("risk", None, "tcol", None),
         P("risk", None),
     )
+    dense = mesh.shape["risk"] == 4 * REINS // RB and mesh.shape["tcol"] == 2
     return jax.shard_map(
-        on_device,
+        dense_on_device if dense else sparse_on_device,
         mesh=mesh,
         in_specs=placed,
         out_specs=(P("tcol", "risk"), P("tcol", "risk")),

time: 231 us -> 80.1 us (0.35)
  waiting for transfers between devices: 163 us -> 34 us
  between operations: 14.2 us -> 0.69 us
  blocking collectives: 2.08 us -> 15.3 us
  local copies, waits for them, and re-layouts: 22.2 us -> 9.04 us
  Pallas kernels: 0 us -> 11.8 us
  matrix products: 10.3 us -> 0 us
  starting transfers between devices: 15.4 us -> 8.53 us
  other arithmetic: 2.93 us -> 0 us
    reduce_scatter x1 -> x0, waiting for transfers between devices: 89.4 us -> none  [on_device(): lax.psum_scatter(retro_terms, 'risk', scatter_dimension=1, tiled=True)]
    all_to_all x2 -> x1, waiting for transfers between devices: 73.6 us -> 32.7 us  [dense_on_device(): lax.all_to_all(outbound, 'risk', split_axis=0, concat_axis=0, tiled=True)]
    all_to_all x0 -> x1, blocking collectives: none -> 15.3 us  [dense_on_device(): lax.all_to_all(pieces, 'risk', split_axis=0, concat_axis=0, tiled=True)]
    pallas_call x0 -> x3, Pallas kernels: none -> 11.8 us  [the longest x1 8.22 us: block_sums(): pl.pallas_call(block_sums_kernel, grid=(steps,), in_specs=[smem, smem, pl...]
    dot_general x5 -> x0, matrix products: 10.3 us -> none  [the longest x1 3.64 us: on_device(): jnp.einsum('sg,syb->ygb', selector, inbound.reshape(-1, years_dev, TB), p...]
    scatter x2 -> x0, local copies, waits for them, and re-layouts: 9.39 us -> none  [the longest x1 8.61 us: on_device(): jnp.zeros((risk_count * capacity, years_dev, TB), jnp.float32).at[slot_id]]
    unnamed x15 -> x28, local copies, waits for them, and re-layouts: 1.05 us -> 9.04 us
    reshape x2 -> x0, local copies, waits for them, and re-layouts: 7.97 us -> none  [the longest x1 7.4 us: on_device(): outbound = outbound.reshape(risk_count, capacity, years_dev, TB)]
  transfers between devices with their start and end apart: 3 -> 2, of which waited for: 2 -> 2; matrix products, arithmetic and copies ran while one was open for 12% -> 0% of each run, Pallas kernels for 0% -> 0%
where the time goes in v1:
time: 80.1 us; the launch traced here: 79.4 us
  waiting for transfers between devices  34 us (42%)
  blocking collectives  15.3 us (19%)
  Pallas kernels  11.8 us (15%)
  local copies, waits for them, and re-layouts  9.04 us (11%)
  starting transfers between devices  8.53 us (11%)
    all_to_all x1, waiting for transfers between devices, dense_on_device(): lax.all_to_all(outbound, 'risk', split_axis=0, concat_axis=0, tiled=True)  32.7 us
    all_to_all x1, blocking collectives, dense_on_device(): lax.all_to_all(pieces, 'risk', split_axis=0, concat_axis=0, tiled=True)  15.3 us
    unnamed x28, local copies, waits for them, and re-layouts  9.04 us
    all_to_all x1, starting transfers between devices, dense_on_device(): lax.all_to_all(outbound, 'risk', split_axis=0, concat_axis=0, tiled=True)  8.46 us
    pallas_call x1, Pallas kernels, block_sums(): pl.pallas_call(block_sums_kernel, grid=(steps,), in_specs=[smem, smem, pl...  8.22 us
    pallas_call x1, Pallas kernels, retro(): pl.pallas_call(retro_kernel, in_specs=[pl.BlockSpec(memory_space=pltpu.SM...  1.97 us
    pallas_call x1, Pallas kernels, finish(): pl.pallas_call(finish_kernel, out_shape=jax.ShapeDtypeStruct((pieces.shap...  1.61 us
  transfers between devices with their start and end apart: 2, of which 2 were waited for; matrix products, arithmetic and copies ran while one was open for 0% of the time, Pallas kernels for 0%

profile of v1, /device:TPU:0, one launch (start us, length us, event | category | flops | bytes accessed | tf_op | source)
XLA Modules:
  0.0 79.4 jit_solution(5436082485927985540)
XLA Ops:
  0.6 0.0 copy-start
  0.6 1.2 %copy-done = bf16[64,8192]{1,0:T(8,128)(2,1)S(1)} copy-done((bf16[64,8192]{1,0:T(8,128)(2,1)S(1)}, bf16[64,8192]{1,0:T(8,128)(2,1)}, u32[]{:S(2)}) %copy-start) | copy-done | bytes 1048600
  1.9 0.0 copy-start.1
  1.9 1.2 %copy-done.1 = bf16[64,8192]{1,0:T(8,128)(2,1)S(1)} copy-done((bf16[64,8192]{1,0:T(8,128)(2,1)S(1)}, bf16[64,8192]{1,0:T(8,128)(2,1)}, u32[]{:S(2)}) %copy-start.1) | copy-done | bytes 1048600
  3.1 0.0 copy-start.3
  3.1 0.8 copy-done.3
  3.8 0.0 copy-start.4
  3.8 0.8 copy-done.4
  4.6 0.0 copy-start.5
  4.6 0.8 copy-done.5
  5.4 0.0 copy-start.6
  5.4 0.8 copy-done.6
  6.1 0.0 copy-start.7
  6.1 0.7 copy-done.7
  6.8 0.0 copy-start.10
  6.8 0.7 copy-done.10
  7.5 0.0 copy-start.11
  7.5 0.7 copy-done.11
  8.1 8.2 %shard_map.140 = s16[96,64,128]{2,1,0:T(8,128)(2,1)} custom-call(s32[64]{0:T(128)S(1)} %bitcast.15, s32[64]{0:T(128)S(1)} %copy-done.11, bf16[64,8192]{1,0:T(8,128)(2,1)S(1)} %copy-done, bf16[64,64]{1,0:T(8,128)(2,1)S(1)} %copy-done.7, bf16[64,8192]{1,0:T(8,128)(2,1)S(1)} %copy-done.1, f32[64,128]{1,0:T(8,128)S(1)} %bitcast.9, f32[64,128]{1,0:T(8,128)S(1)} %bitcast.10, ...), custom_call_target="tpu_custom_call" | custom-call | tf_op jit(solution)/shard_map/pallas_call | solution.py:69
  16.4 0.0 copy-start.2
  16.4 0.0 copy-start.12
  16.4 0.0 copy-start.8
  16.4 0.0 copy-start.9
  16.4 8.5 %all-to-all-start = ((s16[96,64,128]{2,1,0:T(8,128)(2,1)}), s16[96,64,128]{2,1,0:T(8,128)(2,1)S(1)}, u32[]{:S(2)}, u32[]{:S(2)}) async-start(s16[96,64,128]{2,1,0:T(8,128)(2,1)} %shard_map.140), calls=%async_computation | async-start | bytes 3145728 | tf_op jit(solution)/shard_map/all_to_all | solution.py:166
  24.8 0.0 copy-done.2
  24.9 0.1 collective-permute-start
  24.9 0.0 copy-done.12
  24.9 0.1 copy.15.rblock_ref
  25.0 1.3 %collective-permute-done.other_ref = bf16[6,2,64,128]{3,2,1,0:T(8,128)(2,1)S(1)} collective-permute-done((bf16[6,2,64,128]{3,2,1,0:T(8,128)(2,1)S(1)}, bf16[6,2,64,128]{3,2,1,0:T(8,128)(2,1)S(1)}, u32[]{:S(2)}, u32[]{:S(2)}) %collective-permute-start) | collective-permute-done | bytes 196640 | tf_op jit(solution)/shard_map/ppermute | solution.py:161
  26.4 32.7 %all-to-all-done = s16[96,64,128]{2,1,0:T(8,128)(2,1)S(1)} async-done(((s16[96,64,128]{2,1,0:T(8,128)(2,1)}), s16[96,64,128]{2,1,0:T(8,128)(2,1)S(1)}, u32[]{:S(2)}, u32[]{:S(2)}) %all-to-all-start) | async-done | bytes 1572896 | tf_op jit(solution)/shard_map/all_to_all | solution.py:166
  59.0 0.0 copy-done.8
  59.0 0.0 copy-done.9
  59.0 2.0 %shard_map.141 = (f32[64,768]{1,0:T(8,128)}, f32[16,16,128]{2,1,0:T(8,128)S(1)}) custom-call(s32[6,2]{1,0:T(8,128)S(1)} %copy.15.rblock_ref, s16[16,6,64,128]{3,2,1,0:T(8,128)(2,1)S(1)} %bitcast.8, f32[6,128]{1,0:T(8,128)S(1)} %bitcast.13, f32[6,128]{1,0:T(8,128)S(1)} %bitcast.14, bf16[6,2,64,128]{3,2,1,0:T(8,128)(2,1)S(1)} %copy-done.2, ...), custom_call_target="tpu_custom_call" | custom-call | tf_op jit(solution)/shard_map/pallas_call | solution.py:125
  61.0 15.3 %all_to_all.10.in_ref = f32[16,16,128]{2,1,0:T(8,128)} all-to-all(f32[16,16,128]{2,1,0:T(8,128)S(1)} %get-tuple-element.5), channel_id=1, replica_groups=mesh['risk'=16,'tcol'=2] {'risk'}, dimensions={0} | all-to-all | bytes 262144 | tf_op jit(solution)/shard_map/all_to_all | solution.py:169
  76.3 1.6 %shard_map.142 = f32[64,32]{1,0:T(8,128)} custom-call(f32[16,16,128]{2,1,0:T(8,128)} %all_to_all.10.in_ref), custom_call_target="tpu_custom_call" | custom-call | tf_op jit(solution)/shard_map/pallas_call | solution.py:148
  77.9 1.4 %copy.16 = f32[64,32]{0,1:T(8,128)} copy(f32[64,32]{1,0:T(8,128)} %shard_map.142) | data formatting | bytes 16384
Async XLA Ops:
  0.6 1.2 %copy-start = (bf16[64,8192]{1,0:T(8,128)(2,1)S(1)}, bf16[64,8192]{1,0:T(8,128)(2,1)}, u32[]{:S(2)}) copy-start(bf16[64,8192]{1,0:T(8,128)(2,1)} %idio_ref.1) | copy-start | bytes 3145732
  1.9 1.2 %copy-start.1 = (bf16[64,8192]{1,0:T(8,128)(2,1)S(1)}, bf16[64,8192]{1,0:T(8,128)(2,1)}, u32[]{:S(2)}) copy-start(bf16[64,8192]{1,0:T(8,128)(2,1)} %loads_ref.1) | copy-start | bytes 3145732
  3.1 0.8 copy-start.3
  3.8 0.8 copy-start.4
  4.6 0.8 copy-start.5
  5.4 0.8 copy-start.6
  6.1 0.7 copy-start.7
  6.8 0.7 copy-start.10
  7.5 0.7 copy-start.11
  16.4 8.5 %copy-start.2 = (bf16[6,2,64,128]{3,2,1,0:T(8,128)(2,1)S(1)}, bf16[6,2,64,128]{3,2,1,0:T(8,128)(2,1)}, u32[]{:S(2)}) copy-start(bf16[6,2,64,128]{3,2,1,0:T(8,128)(2,1)} %mine_ref.1) | copy-start | bytes 589828
  16.4 8.6 %copy-start.12 = (s32[6,2]{0,1:T(2,128)S(1)}, s32[6,2]{0,1:T(2,128)}, u32[]{:S(2)}) copy-start(s32[6,2]{0,1:T(2,128)} %param.25) | copy-start | bytes 148
  16.4 42.7 %copy-start.8 = (f32[768]{0:T(1024)S(1)}, f32[768]{0:T(1024)}, u32[]{:S(2)}) copy-start(f32[768]{0:T(1024)} %param.22) | copy-start | bytes 9220
  16.4 42.7 %copy-start.9 = (f32[768]{0:T(1024)S(1)}, f32[768]{0:T(1024)}, u32[]{:S(2)}) copy-start(f32[768]{0:T(1024)} %param.23) | copy-start | bytes 9220
  16.4 42.6 %all-to-all-start = ((s16[96,64,128]{2,1,0:T(8,128)(2,1)}), s16[96,64,128]{2,1,0:T(8,128)(2,1)S(1)}, u32[]{:S(2)}, u32[]{:S(2)}) async-start(s16[96,64,128]{2,1,0:T(8,128)(2,1)} %shard_map.140), calls=%async_computation | async-start | bytes 3145728 | tf_op jit(solution)/shard_map/all_to_all | solution.py:166
  24.9 1.5 %collective-permute-start = (bf16[6,2,64,128]{3,2,1,0:T(8,128)(2,1)S(1)}, bf16[6,2,64,128]{3,2,1,0:T(8,128)(2,1)S(1)}, u32[]{:S(2)}, u32[]{:S(2)}) collective-permute-start(bf16[6,2,64,128]{3,2,1,0:T(8,128)(2,1)S(1)} %copy-done.2), channel_id=1, source_target_pairs={{0,1},{1,0},{2,3},{3,2},{4,5},{5,4},{6,7},{7,6},{8,9},{9,8},{10,11... | collective-permute-start | bytes 589832 | tf_op jit(solution)/shard_map/ppermute | solution.py:161

commit v2 on v1

--- a/solution.py
+++ b/solution.py
@@ -1,3 +1,5 @@
+import functools
+
 import jax
 import jax.numpy as jnp
 from jax import lax
@@ -22,17 +24,28 @@
     return (coded.astype(jnp.int32) + HALF).astype(jnp.float32) * (1.0 / SCALE)
 
 
+def relative_code(rel, order):
+    code = 0
+    for bit in order:
+        code = code * 2 + ((rel >> bit) & 1)
+    return code
+
+
 def block_sums_kernel(
-    owner_ref, sub_ref, idio_ref, factor_ref, loads_ref, scale_ref, sigma_ref, weight_ref, slot_ref,
-    out_ref, acc_ref,
+    parts, owned, owner_ref, sub_ref, idio_ref, factor_ref, loads_ref, scale_ref, sigma_ref, weight_ref, slot_ref,
+    *out_refs,
 ):
-    blocks_owned = acc_ref.shape[0] // lax.axis_size("risk")
+    send_refs, keep_refs, high_refs = (out_refs[i * len(parts) : (i + 1) * len(parts)] for i in range(3))
+    half = keep_refs[0].shape[0]
     step = pl.program_id(0)
     tiles = scale_ref.shape[0]
+    me = lax.axis_index("risk")
+    core = lax.axis_index("tcol")
 
     @pl.when(step == 0)
     def _():
-        acc_ref[...] = jnp.zeros_like(acc_ref)
+        for ref in keep_refs + high_refs:
+            ref[...] = jnp.zeros_like(ref)
 
     factor = factor_ref[...]
     rows = lax.broadcasted_iota(jnp.int32, (TB, TB), 0)
@@ -47,27 +60,42 @@
             preferred_element_type=jnp.float32,
         )
         tile = step * tiles + k
-        at = owner_ref[tile] * blocks_owned + sub_ref[tile]
-        acc_ref[at] += sums
+        rel = owner_ref[tile] ^ me
+        for (first, count, order), keep_ref, high_ref in zip(parts, keep_refs, high_refs):
+            code = jnp.where(core == 0, relative_code(rel, order[0]), relative_code(rel, order[1]))
+            at = code * owned + sub_ref[tile]
+            mine = sums[first : first + count]
+
+            @pl.when(at < half)
+            def _():
+                keep_ref[at] += mine
+
+            @pl.when(at >= half)
+            def _():
+                high_ref[at - half] += mine
 
     @pl.when(step == pl.num_programs(0) - 1)
     def _():
-        def body(b, carry):
-            out_ref[b] = encode(acc_ref[b])
-            return carry
-
-        lax.fori_loop(0, acc_ref.shape[0], body, 0, unroll=4)
-
-
-def block_sums(idio, factor, loads, log_scale, sigma, weight, slot, owner, sub, blocks, steps=4):
+        for send_ref, high_ref in zip(send_refs, high_refs):
+
+            def body(b, carry):
+                send_ref[b] = encode(high_ref[b])
+                return carry
+
+            lax.fori_loop(0, half, body, 0, unroll=4)
+
+
+def block_sums(parts, idio, factor, loads, log_scale, sigma, weight, slot, owner, sub, blocks, owned, steps=4):
     years, risks = idio.shape
     tiles = sub.shape[0]
     per = tiles // steps
     fold = lambda a: a.reshape(tiles, TB)
     row = pl.BlockSpec((per, TB), lambda i: (i, 0))
     smem = pl.BlockSpec(memory_space=pltpu.SMEM)
-    return pl.pallas_call(
-        block_sums_kernel,
+    shapes = [(blocks // 2, count, TB) for _, count, _ in parts]
+    whole = [pl.BlockSpec(s, lambda i: (0, 0, 0)) for s in shapes]
+    out = pl.pallas_call(
+        functools.partial(block_sums_kernel, parts, owned),
         grid=(steps,),
         in_specs=[
             smem,
@@ -80,22 +108,30 @@
             row,
             row,
         ],
-        out_specs=pl.BlockSpec((blocks, years, TB), lambda i: (0, 0, 0)),
-        out_shape=jax.ShapeDtypeStruct((blocks, years, TB), jnp.int16),
-        scratch_shapes=[pltpu.VMEM((blocks, years, TB), jnp.float32)],
-        compiler_params=pltpu.CompilerParams(vmem_limit_bytes=40 * 2**20),
+        out_specs=whole * 2,
+        out_shape=[jax.ShapeDtypeStruct(s, jnp.int16) for s in shapes]
+        + [jax.ShapeDtypeStruct(s, jnp.float32) for s in shapes],
+        scratch_shapes=[pltpu.VMEM(s, jnp.float32) for s in shapes],
+        compiler_params=pltpu.CompilerParams(vmem_limit_bytes=60 * 2**20),
     )(owner.reshape(-1), sub, idio, factor, loads, fold(log_scale), fold(sigma), fold(weight), fold(slot))
-
-
-def retro_kernel(rblock_ref, inbound_ref, attach_ref, limit_ref, mine_ref, other_ref, ceded_ref, out_ref, acc_ref):
-    sources, owned, years, _ = inbound_ref.shape
-    tiles = mine_ref.shape[1]
+    return out[: len(parts)], out[len(parts) :]
+
+
+def retro_kernel(parts, rblock_ref, attach_ref, limit_ref, mine_ref, other_ref, *refs):
+    *in_refs, ceded_ref, out_ref, acc_ref = refs
+    each = len(in_refs) // len(parts)
+    owned, tiles = mine_ref.shape[:2]
     first = lax.axis_index("tcol") == 0
     acc_ref[...] = jnp.zeros_like(acc_ref)
     for g in range(owned):
-        gross = decode(inbound_ref[0, g])
-        for s in range(1, sources):
-            gross += decode(inbound_ref[s, g])
+        sums = []
+        for p in range(len(parts)):
+            gross, *inbound = in_refs[p * each : (p + 1) * each]
+            total = gross[g]
+            for ref in inbound:
+                total += decode(ref[g])
+            sums.append(total)
+        gross = jnp.concatenate(sums, axis=0)
         ceded = jnp.minimum(jnp.maximum(gross - attach_ref[pl.ds(g, 1), :], 0.0), limit_ref[pl.ds(g, 1), :])
         ceded_ref[:, pl.ds(g * TB, TB)] = ceded
         low = ceded.astype(jnp.bfloat16)
@@ -103,52 +139,59 @@
             mine, other = mine_ref[g, k], other_ref[g, k]
             top = jnp.where(first, mine, other)
             bottom = jnp.where(first, other, mine)
-            part = jnp.dot(low, jnp.concatenate([top, bottom], axis=0), preferred_element_type=jnp.float32)
+            part = lax.dot_general(
+                jnp.concatenate([top, bottom], axis=0), low, (((0,), (1,)), ((), ())),
+                preferred_element_type=jnp.float32,
+            )
             acc_ref[rblock_ref[g, k]] += part
     wide = RB // 4
-    quarter = years // 4
-    lane = lax.broadcasted_iota(jnp.int32, (quarter, RB), 1) // wide
     for q in range(acc_ref.shape[0]):
-        parts = [acc_ref[q, pl.ds(j * quarter, quarter), :] for j in range(4)]
         for i in range(4):
-            packed = parts[i]
-            for j in range(4):
-                if j != i:
-                    moved = pltpu.roll(parts[j], ((j - i) * wide) % RB, 1)
-                    packed = jnp.where(lane == j, moved, packed)
-            out_ref[4 * q + i] = packed
-
-
-def retro(inbound, attach, limit, mine, other, rblock):
-    sources, owned, years, _ = inbound.shape
+            for h in range(2):
+                out_ref[4 * q + i, :, h * 64 : (h + 1) * 64] = acc_ref[q, pl.ds(i * wide + h * wide // 2, wide // 2), :]
+
+
+def retro(parts, inbound, attach, limit, mine, other, rblock):
+    owned = mine.shape[0]
+    years = sum(count for _, count, _ in parts)
     vmem = pl.BlockSpec(memory_space=pltpu.VMEM)
+    whole = lambda a: pl.BlockSpec(a.shape, lambda i: (0,) * a.ndim)
+    first = lambda a: pl.BlockSpec((owned,) + a.shape[1:], lambda i: (0, 0, 0))
+    attach, limit = attach.reshape(owned, TB), limit.reshape(owned, TB)
+    outs = [
+        jax.ShapeDtypeStruct((years, owned * TB), jnp.float32),
+        jax.ShapeDtypeStruct((REINS * 4 // RB, RB // 8, RB), jnp.float32),
+    ]
     return pl.pallas_call(
-        retro_kernel,
-        in_specs=[pl.BlockSpec(memory_space=pltpu.SMEM)] + [vmem] * 5,
-        out_specs=[vmem, vmem],
-        out_shape=[
-            jax.ShapeDtypeStruct((years, owned * TB), jnp.float32),
-            jax.ShapeDtypeStruct((REINS * 4 // RB, years // 4, RB), jnp.float32),
-        ],
-        scratch_shapes=[pltpu.VMEM((REINS // RB, years, RB), jnp.float32)],
-        compiler_params=pltpu.CompilerParams(vmem_limit_bytes=40 * 2**20),
-    )(rblock, inbound, attach.reshape(owned, TB), limit.reshape(owned, TB), mine, other)
+        functools.partial(retro_kernel, parts),
+        grid=(1,),
+        in_specs=[pl.BlockSpec(memory_space=pltpu.SMEM)]
+        + [whole(a) for a in (attach, limit, mine, other)]
+        + [first(a) for a in inbound],
+        out_specs=[whole(a) for a in outs],
+        out_shape=outs,
+        scratch_shapes=[pltpu.VMEM((REINS // RB, RB, years), jnp.float32)],
+        compiler_params=pltpu.CompilerParams(vmem_limit_bytes=20 * 2**20),
+    )(rblock, attach, limit, mine, other, *inbound)
 
 
 def finish_kernel(in_ref, out_ref):
     total = in_ref[0]
     for s in range(1, in_ref.shape[0]):
         total += in_ref[s]
-    quarter, wide = total.shape[0], RB // 4
-    for j in range(4):
-        out_ref[pl.ds(j * quarter, quarter), :] = total[:, j * wide : (j + 1) * wide]
+    half, years = out_ref.shape[0] // 2, out_ref.shape[1]
+    for h in range(2):
+        out_ref[pl.ds(h * half, half), :] = total[:, h * years : (h + 1) * years]
 
 
 def finish(pieces):
     return pl.pallas_call(
         finish_kernel,
-        out_shape=jax.ShapeDtypeStruct((pieces.shape[1] * 4, RB // 4), jnp.float32),
-    )(pieces)
+        out_shape=jax.ShapeDtypeStruct((RB // 4, 2 * RB // 4), jnp.float32),
+    )(pieces).T
+
+
+PARTS = ((0, 64, ((0, 1, 2, 3), (1, 0, 2, 3))),)
 
 
 def dense_on_device(
@@ -156,16 +199,31 @@
     tile_owner, tile_sub, attach, limit, share_values, share_rblock,
 ):
     risk_count = lax.axis_size("risk")
-    years_dev = idio_normals.shape[0]
     owned = attach.shape[0] // TB
     other_shares = lax.ppermute(share_values, "tcol", [(0, 1), (1, 0)])
-    outbound = block_sums(
-        idio_normals, factor_normals, loadings, log_scale, sigma, idio_weight, risk_slot,
-        tile_owner, tile_sub, risk_count * owned,
-    )
-    inbound = lax.all_to_all(outbound, "risk", split_axis=0, concat_axis=0, tiled=True)
-    inbound = inbound.reshape(risk_count, owned, years_dev, TB)
-    ceded, pieces = retro(inbound, attach, limit, share_values, other_shares, share_rblock)
+    sends, keeps = block_sums(
+        PARTS, idio_normals, factor_normals, loadings, log_scale, sigma, idio_weight, risk_slot,
+        tile_owner, tile_sub, risk_count * owned, owned,
+    )
+    received = [[keep] for keep in keeps]
+    sends = list(sends)
+    steps = len(PARTS[0][2][0])
+    count = keeps[0].shape[0]
+    for step in range(steps):
+        for p, (_, _, order) in enumerate(PARTS):
+            pairs = [
+                (2 * r + c, 2 * (r ^ (1 << order[c][step])) + c) for r in range(risk_count) for c in range(2)
+            ]
+            received[p].append(lax.ppermute(sends[p], ("risk", "tcol"), pairs))
+        if step < steps - 1:
+            count //= 2
+            for p in range(len(PARTS)):
+                total, *inbound = [a[count : 2 * count] for a in received[p]]
+                for a in inbound:
+                    total += decode(a)
+                sends[p] = encode(total)
+    inbound = [a for arrays in received for a in arrays]
+    ceded, pieces = retro(PARTS, inbound, attach, limit, share_values, other_shares, share_rblock)
     pieces = lax.all_to_all(pieces, "risk", split_axis=0, concat_axis=0, tiled=True)
     return ceded, finish(pieces)
 

time: 80.1 us -> 74.3 us (0.928)
  waiting for transfers between devices: 34 us -> 22.1 us
  Pallas kernels: 11.8 us -> 22.9 us
  local copies, waits for them, and re-layouts: 9.04 us -> 0.11 us
  starting transfers between devices: 8.53 us -> 10.6 us
  other arithmetic: 0 us -> 2 us
    all_to_all x1 -> x0, waiting for transfers between devices: 32.7 us -> none  [dense_on_device(): lax.all_to_all(outbound, 'risk', split_axis=0, concat_axis=0, tiled=True)]
    ppermute x0 -> x4, waiting for transfers between devices: none -> 22.1 us  [dense_on_device(): received[p].append(lax.ppermute(sends[p], ('risk', 'tcol'), pairs))]
    pallas_call x3, Pallas kernels: 11.8 us -> 22.9 us  [the longest x1 19.8 us: block_sums(): pl.pallas_call(functools.partial(block_sums_kernel, parts, owned), grid=(...]
    ppermute x0 -> x4, starting transfers between devices: none -> 10.6 us  [dense_on_device(): received[p].append(lax.ppermute(sends[p], ('risk', 'tcol'), pairs))]
    unnamed x28 -> x11, local copies, waits for them, and re-layouts: 9.04 us -> 0.11 us
    all_to_all x1 -> x0, starting transfers between devices: 8.46 us -> none  [dense_on_device(): lax.all_to_all(outbound, 'risk', split_axis=0, concat_axis=0, tiled=True)]
    convert_element_type x0 -> x3, other arithmetic: none -> 2 us  [encode(): return steps.astype(jnp.int16)]
    ppermute x1, waiting for transfers between devices: 1.32 us -> 0.01 us  [dense_on_device(): other_shares = lax.ppermute(share_values, 'tcol', [(0, 1), (1, 0)])]
  transfers between devices with their start and end apart: 2 -> 5, of which waited for: 2 -> 4; matrix products, arithmetic and copies ran while one was open for 0% -> 0% of each run, Pallas kernels for 0% -> 0%
where the time goes in v2:
time: 74.3 us; the launch traced here: 74.1 us
  Pallas kernels  22.9 us (31%)
  waiting for transfers between devices  22.1 us (30%)
  blocking collectives  15.7 us (21%)
  starting transfers between devices  10.6 us (14%)
  other arithmetic  2 us (3%)
    ppermute x4, waiting for transfers between devices, dense_on_device(): received[p].append(lax.ppermute(sends[p], ('risk', 'tcol'), pairs))  22.1 us
    pallas_call x1, Pallas kernels, block_sums(): pl.pallas_call(functools.partial(block_sums_kernel, parts, owned), grid=(...  19.8 us
    all_to_all x1, blocking collectives, dense_on_device(): lax.all_to_all(pieces, 'risk', split_axis=0, concat_axis=0, tiled=True)  15.7 us
    ppermute x4, starting transfers between devices, dense_on_device(): received[p].append(lax.ppermute(sends[p], ('risk', 'tcol'), pairs))  10.6 us
    convert_element_type x3, other arithmetic, encode(): return steps.astype(jnp.int16)  2 us
    pallas_call x1, Pallas kernels, retro(): pl.pallas_call(functools.partial(retro_kernel, parts), grid=(1,), in_spec...  1.6 us
    pallas_call x1, Pallas kernels, finish(): pl.pallas_call(finish_kernel, out_shape=jax.ShapeDtypeStruct((RB // 4, 2...  1.59 us
  transfers between devices with their start and end apart: 5, of which 4 were waited for; matrix products, arithmetic and copies ran while one was open for 0% of the time, Pallas kernels for 0%

profile of v2, /device:TPU:0, one launch (start us, length us, event | category | flops | bytes accessed | tf_op | source)
XLA Modules:
  0.0 74.1 jit_solution(5656516594829372623)
XLA Ops:
  0.6 19.8 %shard_map.140 = (s16[48,64,128]{2,1,0:T(8,128)(2,1)}, f32[48,64,128]{2,1,0:T(8,128)}) custom-call(s32[64]{0:T(128)} %bitcast.15, s32[64]{0:T(128)} %sub_ref.1, bf16[64,8192]{1,0:T(8,128)(2,1)} %idio_ref.1, bf16[64,64]{1,0:T(8,128)(2,1)} %factor_ref.1, bf16[64,8192]{1,0:T(8,128)(2,1)} %loads_ref.1, f32[64,128]{1,0:T(8,128)} %bitcast.10, f32[64,128]{1,0:T(8,128)} %bitcast.11, ...), custom_call_target="tpu_custom_call" | custom-call | tf_op jit(solution)/shard_map/pallas_call | solution.py:97
  20.4 0.0 copy-start
  20.4 0.0 copy-start.1
  20.4 3.0 %collective-permute-start.1 = (s16[48,64,128]{2,1,0:T(8,128)(2,1)}, s16[48,64,128]{2,1,0:T(8,128)(2,1)S(1)}, u32[]{:S(2)}, u32[]{:S(2)}) collective-permute-start(s16[48,64,128]{2,1,0:T(8,128)(2,1)} %get-tuple-element.7), channel_id=1, source_target_pairs={{0,2},{1,5},{2,0},{3,7},{4,6},{5,1},{6,4},{7,3},{8,10},{9,13},{10,... | collective-permute-start | bytes 2359304 | tf_op jit(solution)/shard_map/ppermute | solution.py:217
  23.4 10.2 %collective-permute-done.1.refs_1_ = s16[48,64,128]{2,1,0:T(8,128)(2,1)S(1)} collective-permute-done((s16[48,64,128]{2,1,0:T(8,128)(2,1)}, s16[48,64,128]{2,1,0:T(8,128)(2,1)S(1)}, u32[]{:S(2)}, u32[]{:S(2)}) %collective-permute-start.1) | collective-permute-done | bytes 786464 | tf_op jit(solution)/shard_map/ppermute | solution.py:217
  33.6 0.0 copy-start.4
  33.6 0.0 copy-start.2
  33.6 0.0 copy-start.3
  33.6 1.5 %add_convert_fusion = s16[24,64,128]{2,1,0:T(8,128)(2,1)S(1)} fusion(f32[48,64,128]{2,1,0:T(8,128)} %get-tuple-element.6.refs_0_, s16[48,64,128]{2,1,0:T(8,128)(2,1)S(1)} %collective-permute-done.1.refs_1_), kind=kLoop, calls=%fused_computation | loop fusion | flops 2162688 | bytes 1572864 | tf_op jit(solution)/shard_map/convert_element_type | solution.py:20
  35.1 2.1 %collective-permute-start.2 = (s16[24,64,128]{2,1,0:T(8,128)(2,1)S(1)}, s16[24,64,128]{2,1,0:T(8,128)(2,1)S(1)}, u32[]{:S(2)}, u32[]{:S(2)}) collective-permute-start(s16[24,64,128]{2,1,0:T(8,128)(2,1)S(1)} %add_convert_fusion), channel_id=1, source_target_pairs={{0,4},{1,3},{2,6},{3,1},{4,0},{5,7},{6,2},{7,5},{8,12},{9,11},{10,... | collective-permute-start | bytes 1179656 | tf_op jit(solution)/shard_map/ppermute | solution.py:217
  37.2 5.8 %collective-permute-done.2.refs_2_ = s16[24,64,128]{2,1,0:T(8,128)(2,1)S(1)} collective-permute-done((s16[24,64,128]{2,1,0:T(8,128)(2,1)S(1)}, s16[24,64,128]{2,1,0:T(8,128)(2,1)S(1)}, u32[]{:S(2)}, u32[]{:S(2)}) %collective-permute-start.2) | collective-permute-done | bytes 393248 | tf_op jit(solution)/shard_map/ppermute | solution.py:217
  43.0 0.0 copy-done
  43.0 0.3 add_convert_fusion.1
  43.3 2.1 %collective-permute-start.3 = (s16[12,64,128]{2,1,0:T(8,128)(2,1)S(1)}, s16[12,64,128]{2,1,0:T(8,128)(2,1)S(1)}, u32[]{:S(2)}, u32[]{:S(2)}) collective-permute-start(s16[12,64,128]{2,1,0:T(8,128)(2,1)S(1)} %add_convert_fusion.1), channel_id=1, source_target_pairs={{0,8},{1,9},{2,10},{3,11},{4,12},{5,13},{6,14},{7,15},{8,0},{9,1},... | collective-permute-start | bytes 589832 | tf_op jit(solution)/shard_map/ppermute | solution.py:217
  45.4 0.0 copy-done.1
  45.4 0.0 collective-permute-start
  45.4 3.6 %collective-permute-done.3.refs_3_ = s16[12,64,128]{2,1,0:T(8,128)(2,1)S(1)} collective-permute-done((s16[12,64,128]{2,1,0:T(8,128)(2,1)S(1)}, s16[12,64,128]{2,1,0:T(8,128)(2,1)S(1)}, u32[]{:S(2)}, u32[]{:S(2)}) %collective-permute-start.3) | collective-permute-done | bytes 196640 | tf_op jit(solution)/shard_map/ppermute | solution.py:217
  49.1 0.2 add_convert_fusion.2
  49.3 3.3 %collective-permute-start.4 = (s16[6,64,128]{2,1,0:T(8,128)(2,1)S(1)}, s16[6,64,128]{2,1,0:T(8,128)(2,1)S(1)}, u32[]{:S(2)}, u32[]{:S(2)}) collective-permute-start(s16[6,64,128]{2,1,0:T(8,128)(2,1)S(1)} %add_convert_fusion.2), channel_id=1, source_target_pairs={{0,16},{1,17},{2,18},{3,19},{4,20},{5,21},{6,22},{7,23},{8,24},{9,... | collective-permute-start | bytes 294920 | tf_op jit(solution)/shard_map/ppermute | solution.py:217
  52.6 0.0 copy-done.4
  52.6 0.1 copy.15.rblock_ref
  52.7 0.0 collective-permute-done.other_ref
  52.7 2.5 %collective-permute-done.4.refs_4_ = s16[6,64,128]{2,1,0:T(8,128)(2,1)S(1)} collective-permute-done((s16[6,64,128]{2,1,0:T(8,128)(2,1)S(1)}, s16[6,64,128]{2,1,0:T(8,128)(2,1)S(1)}, u32[]{:S(2)}, u32[]{:S(2)}) %collective-permute-start.4) | collective-permute-done | bytes 98336 | tf_op jit(solution)/shard_map/ppermute | solution.py:217
  55.2 0.0 copy-done.2
  55.2 0.0 copy-done.3
  55.2 1.6 %shard_map.141 = (f32[64,768]{1,0:T(8,128)}, f32[16,16,128]{2,1,0:T(8,128)S(1)}) custom-call(s32[6,2]{1,0:T(8,128)S(1)} %copy.15.rblock_ref, f32[6,128]{1,0:T(8,128)S(1)} %bitcast.8, f32[6,128]{1,0:T(8,128)S(1)} %bitcast.9, bf16[6,2,64,128]{3,2,1,0:T(8,128)(2,1)S(1)} %copy-done.1, bf16[6,2,64,128]{3,2,1,0:T(8,128)(2,1)S(1)} %collective-permute-done.other_ref, ...), custom_call_target="tpu_custom_call" | custom-call | tf_op jit(solution)/shard_map/pallas_call | solution.py:165
  56.8 15.7 %all_to_all.5.in_ref = f32[16,16,128]{2,1,0:T(8,128)} all-to-all(f32[16,16,128]{2,1,0:T(8,128)S(1)} %get-tuple-element.9), channel_id=1, replica_groups=mesh['risk'=16,'tcol'=2] {'risk'}, dimensions={0} | all-to-all | bytes 262144 | tf_op jit(solution)/shard_map/all_to_all | solution.py:227
  72.5 1.6 %shard_map.142 = f32[32,64]{1,0:T(8,128)} custom-call(f32[16,16,128]{2,1,0:T(8,128)} %all_to_all.5.in_ref), custom_call_target="tpu_custom_call" | custom-call | tf_op jit(solution)/shard_map/pallas_call | solution.py:188
Async XLA Ops:
  20.4 22.6 %copy-start = (f32[48,64,128]{2,1,0:T(8,128)S(1)}, f32[48,64,128]{2,1,0:T(8,128)}, u32[]{:S(2)}) copy-start(f32[48,64,128]{2,1,0:T(8,128)} %get-tuple-element.6.refs_0_) | copy-start | bytes 4718596
  20.4 25.0 %copy-start.1 = (bf16[6,2,64,128]{3,2,1,0:T(8,128)(2,1)S(1)}, bf16[6,2,64,128]{3,2,1,0:T(8,128)(2,1)}, u32[]{:S(2)}) copy-start(bf16[6,2,64,128]{3,2,1,0:T(8,128)(2,1)} %mine_ref.1) | copy-start | bytes 589828
  20.4 13.2 %collective-permute-start.1 = (s16[48,64,128]{2,1,0:T(8,128)(2,1)}, s16[48,64,128]{2,1,0:T(8,128)(2,1)S(1)}, u32[]{:S(2)}, u32[]{:S(2)}) collective-permute-start(s16[48,64,128]{2,1,0:T(8,128)(2,1)} %get-tuple-element.7), channel_id=1, source_target_pairs={{0,2},{1,5},{2,0},{3,7},{4,6},{5,1},{6,4},{7,3},{8,10},{9,13},{10,... | collective-permute-start | bytes 2359304 | tf_op jit(solution)/shard_map/ppermute | solution.py:217
  33.6 19.0 %copy-start.4 = (s32[6,2]{0,1:T(2,128)S(1)}, s32[6,2]{0,1:T(2,128)}, u32[]{:S(2)}) copy-start(s32[6,2]{0,1:T(2,128)} %param.25) | copy-start | bytes 148
  33.6 21.6 %copy-start.2 = (f32[768]{0:T(1024)S(1)}, f32[768]{0:T(1024)}, u32[]{:S(2)}) copy-start(f32[768]{0:T(1024)} %param.22) | copy-start | bytes 9220
  33.6 21.6 %copy-start.3 = (f32[768]{0:T(1024)S(1)}, f32[768]{0:T(1024)}, u32[]{:S(2)}) copy-start(f32[768]{0:T(1024)} %param.23) | copy-start | bytes 9220
  35.1 7.9 %collective-permute-start.2 = (s16[24,64,128]{2,1,0:T(8,128)(2,1)S(1)}, s16[24,64,128]{2,1,0:T(8,128)(2,1)S(1)}, u32[]{:S(2)}, u32[]{:S(2)}) collective-permute-start(s16[24,64,128]{2,1,0:T(8,128)(2,1)S(1)} %add_convert_fusion), channel_id=1, source_target_pairs={{0,4},{1,3},{2,6},{3,1},{4,0},{5,7},{6,2},{7,5},{8,12},{9,11},{10,... | collective-permute-start | bytes 1179656 | tf_op jit(solution)/shard_map/ppermute | solution.py:217
  43.3 5.8 %collective-permute-start.3 = (s16[12,64,128]{2,1,0:T(8,128)(2,1)S(1)}, s16[12,64,128]{2,1,0:T(8,128)(2,1)S(1)}, u32[]{:S(2)}, u32[]{:S(2)}) collective-permute-start(s16[12,64,128]{2,1,0:T(8,128)(2,1)S(1)} %add_convert_fusion.1), channel_id=1, source_target_pairs={{0,8},{1,9},{2,10},{3,11},{4,12},{5,13},{6,14},{7,15},{8,0},{9,1},... | collective-permute-start | bytes 589832 | tf_op jit(solution)/shard_map/ppermute | solution.py:217
  45.4 7.3 %collective-permute-start = (bf16[6,2,64,128]{3,2,1,0:T(8,128)(2,1)S(1)}, bf16[6,2,64,128]{3,2,1,0:T(8,128)(2,1)S(1)}, u32[]{:S(2)}, u32[]{:S(2)}) collective-permute-start(bf16[6,2,64,128]{3,2,1,0:T(8,128)(2,1)S(1)} %copy-done.1), channel_id=1, source_target_pairs={{0,1},{1,0},{2,3},{3,2},{4,5},{5,4},{6,7},{7,6},{8,9},{9,8},{10,11... | collective-permute-start | bytes 589832 | tf_op jit(solution)/shard_map/ppermute | solution.py:203
  49.3 5.9 %collective-permute-start.4 = (s16[6,64,128]{2,1,0:T(8,128)(2,1)S(1)}, s16[6,64,128]{2,1,0:T(8,128)(2,1)S(1)}, u32[]{:S(2)}, u32[]{:S(2)}) collective-permute-start(s16[6,64,128]{2,1,0:T(8,128)(2,1)S(1)} %add_convert_fusion.2), channel_id=1, source_target_pairs={{0,16},{1,17},{2,18},{3,19},{4,20},{5,21},{6,22},{7,23},{8,24},{9,... | collective-permute-start | bytes 294920 | tf_op jit(solution)/shard_map/ppermute | solution.py:217

commit v3 on v2

--- a/solution.py
+++ b/solution.py
@@ -13,6 +13,7 @@
 TOP = 40.0
 SCALE = 65535.0 / TOP
 HALF = 32768
+VMEM_SUMS = 56
 
 
 def encode(sums):
@@ -20,8 +21,13 @@
     return steps.astype(jnp.int16)
 
 
-def decode(coded):
-    return (coded.astype(jnp.int32) + HALF).astype(jnp.float32) * (1.0 / SCALE)
+def decode(*coded):
+    return sum(a.astype(jnp.int32) + HALF for a in coded).astype(jnp.float32) * (1.0 / SCALE)
+
+
+def add_coded(*coded):
+    steps = sum(a.astype(jnp.int32) for a in coded) + (len(coded) - 1) * HALF
+    return jnp.minimum(steps, HALF - 1).astype(jnp.int16)
 
 
 def relative_code(rel, order):
@@ -31,89 +37,106 @@
     return code
 
 
-def block_sums_kernel(
-    parts, owned, owner_ref, sub_ref, idio_ref, factor_ref, loads_ref, scale_ref, sigma_ref, weight_ref, slot_ref,
-    *out_refs,
-):
-    send_refs, keep_refs, high_refs = (out_refs[i * len(parts) : (i + 1) * len(parts)] for i in range(3))
+def block_sums_kernel(parts, owned, chunks, *refs):
+    count = len(parts)
+    in_refs, refs = refs[:9], refs[9:]
+    send_refs, keep_refs, sum_refs, coded_refs = (refs[i * count : (i + 1) * count] for i in range(4))
+    *held, small_sems, sems, out_sems = refs[4 * count :]
+    owner_ref, sub_ref, factor_ref, scale_ref, sigma_ref, weight_ref, slot_ref, idio_ref, loads_ref = held
     half = keep_refs[0].shape[0]
-    step = pl.program_id(0)
     tiles = scale_ref.shape[0]
+    per = tiles // chunks
     me = lax.axis_index("risk")
     core = lax.axis_index("tcol")
 
-    @pl.when(step == 0)
-    def _():
-        for ref in keep_refs + high_refs:
-            ref[...] = jnp.zeros_like(ref)
+    def copies(i):
+        cols = pl.ds(i * per * TB, per * TB)
+        return [
+            pltpu.make_async_copy(source.at[:, cols], target.at[:, cols], sems.at[j, i])
+            for j, (source, target) in enumerate(zip(in_refs[7:], held[7:]))
+        ]
+
+    small = [
+        pltpu.make_async_copy(source, target, small_sems.at[j])
+        for j, (source, target) in enumerate(zip(in_refs[:7], held[:7]))
+    ]
+    for copy in small + [copy for i in range(chunks) for copy in copies(i)]:
+        copy.start()
+    for ref in sum_refs:
+        ref[...] = jnp.zeros_like(ref)
+    for copy in small:
+        copy.wait()
 
     factor = factor_ref[...]
     rows = lax.broadcasted_iota(jnp.int32, (TB, TB), 0)
-    for k in range(tiles):
-        cols = pl.ds(k * TB, TB)
-        common = jnp.dot(factor, loads_ref[:, cols], preferred_element_type=jnp.float32)
-        latent = common + weight_ref[pl.ds(k, 1), :] * idio_ref[:, cols].astype(jnp.float32)
-        losses = jnp.exp(scale_ref[pl.ds(k, 1), :] + sigma_ref[pl.ds(k, 1), :] * latent)
-        chosen = (rows == slot_ref[pl.ds(k, 1), :]).astype(jnp.float32).astype(jnp.bfloat16)
-        sums = lax.dot_general(
-            losses.astype(jnp.bfloat16), chosen, (((1,), (1,)), ((), ())),
-            preferred_element_type=jnp.float32,
-        )
-        tile = step * tiles + k
-        rel = owner_ref[tile] ^ me
-        for (first, count, order), keep_ref, high_ref in zip(parts, keep_refs, high_refs):
-            code = jnp.where(core == 0, relative_code(rel, order[0]), relative_code(rel, order[1]))
-            at = code * owned + sub_ref[tile]
-            mine = sums[first : first + count]
-
-            @pl.when(at < half)
-            def _():
-                keep_ref[at] += mine
-
-            @pl.when(at >= half)
-            def _():
-                high_ref[at - half] += mine
-
-    @pl.when(step == pl.num_programs(0) - 1)
-    def _():
-        for send_ref, high_ref in zip(send_refs, high_refs):
+
+    for i in range(chunks):
+        for copy in copies(i):
+            copy.wait()
+        for j in range(i * per, (i + 1) * per, GROUP):
+            common = jnp.dot(factor, loads_ref[:, pl.ds(j * TB, GROUP * TB)], preferred_element_type=jnp.float32)
+            group = []
+            for k in range(j, j + GROUP):
+                noise = idio_ref[:, pl.ds(k * TB, TB)].astype(jnp.float32)
+                latent = common[:, (k - j) * TB : (k - j + 1) * TB] + weight_ref[pl.ds(k, 1), :] * noise
+                losses = jnp.exp(scale_ref[pl.ds(k, 1), :] + sigma_ref[pl.ds(k, 1), :] * latent)
+                group.append(losses.astype(jnp.bfloat16))
+            for k, losses in zip(range(j, j + GROUP), group):
+                chosen = (rows == slot_ref[pl.ds(k, 1), :]).astype(jnp.float32).astype(jnp.bfloat16)
+                sums = lax.dot_general(
+                    losses, chosen, (((1,), (1,)), ((), ())), preferred_element_type=jnp.float32
+                )
+                rel = owner_ref[k] ^ me
+                for (first, years, order), sum_ref in zip(parts, sum_refs):
+                    code = jnp.where(core == 0, relative_code(rel, order[0]), relative_code(rel, order[1]))
+                    sum_ref[code * owned + sub_ref[k]] += sums[first : first + years]
+
+    out = []
+    piece = half // PIECES
+    for i in range(PIECES):
+        at = pl.ds(i * piece, piece)
+        for p, (send_ref, keep_ref, sum_ref, coded_ref) in enumerate(zip(send_refs, keep_refs, sum_refs, coded_refs)):
 
             def body(b, carry):
-                send_ref[b] = encode(high_ref[b])
+                coded_ref[b] = encode(sum_ref[b])
+                coded_ref[half + b] = encode(sum_ref[half + b])
                 return carry
 
-            lax.fori_loop(0, half, body, 0, unroll=4)
-
-
-def block_sums(parts, idio, factor, loads, log_scale, sigma, weight, slot, owner, sub, blocks, owned, steps=4):
-    years, risks = idio.shape
+            lax.fori_loop(i * piece, (i + 1) * piece, body, 0, unroll=2)
+            for j, (source, target) in enumerate(((coded_ref.at[pl.ds(half + i * piece, piece)], send_ref), (coded_ref.at[at], keep_ref))):
+                copy = pltpu.make_async_copy(source, target.at[at], out_sems.at[p, i, j])
+                copy.start()
+                out.append(copy)
+    for copy in out:
+        copy.wait()
+
+
+GROUP = 16
+PIECES = 2
+
+
+def block_sums(parts, idio, factor, loads, log_scale, sigma, weight, slot, owner, sub, blocks, owned, chunks=2):
     tiles = sub.shape[0]
-    per = tiles // steps
     fold = lambda a: a.reshape(tiles, TB)
-    row = pl.BlockSpec((per, TB), lambda i: (i, 0))
-    smem = pl.BlockSpec(memory_space=pltpu.SMEM)
-    shapes = [(blocks // 2, count, TB) for _, count, _ in parts]
-    whole = [pl.BlockSpec(s, lambda i: (0, 0, 0)) for s in shapes]
+    hbm = pl.BlockSpec(memory_space=pltpu.HBM)
+    shapes = [(blocks // 2, years, TB) for _, years, _ in parts]
+    inputs = (owner.reshape(-1), sub, factor, fold(log_scale), fold(sigma), fold(weight), fold(slot), idio, loads)
     out = pl.pallas_call(
-        functools.partial(block_sums_kernel, parts, owned),
-        grid=(steps,),
-        in_specs=[
-            smem,
-            smem,
-            pl.BlockSpec((years, per * TB), lambda i: (0, i)),
-            pl.BlockSpec(factor.shape, lambda i: (0, 0)),
-            pl.BlockSpec((loads.shape[0], per * TB), lambda i: (0, i)),
-            row,
-            row,
-            row,
-            row,
+        functools.partial(block_sums_kernel, parts, owned, chunks),
+        in_specs=[hbm] * len(inputs),
+        out_specs=[hbm] * (2 * len(parts)),
+        out_shape=[jax.ShapeDtypeStruct(s, jnp.int16) for s in shapes * 2],
+        scratch_shapes=[pltpu.VMEM((blocks, years, TB), jnp.float32) for _, years, _ in parts]
+        + [pltpu.VMEM((blocks, years, TB), jnp.int16) for _, years, _ in parts]
+        + [pltpu.SMEM(a.shape, a.dtype) for a in inputs[:2]]
+        + [pltpu.VMEM(a.shape, a.dtype) for a in inputs[2:]]
+        + [
+            pltpu.SemaphoreType.DMA((7,)),
+            pltpu.SemaphoreType.DMA((2, chunks)),
+            pltpu.SemaphoreType.DMA((len(parts), PIECES, 2)),
         ],
-        out_specs=whole * 2,
-        out_shape=[jax.ShapeDtypeStruct(s, jnp.int16) for s in shapes]
-        + [jax.ShapeDtypeStruct(s, jnp.float32) for s in shapes],
-        scratch_shapes=[pltpu.VMEM(s, jnp.float32) for s in shapes],
-        compiler_params=pltpu.CompilerParams(vmem_limit_bytes=60 * 2**20),
-    )(owner.reshape(-1), sub, idio, factor, loads, fold(log_scale), fold(sigma), fold(weight), fold(slot))
+        compiler_params=pltpu.CompilerParams(vmem_limit_bytes=VMEM_SUMS * 2**20),
+    )(*inputs)
     return out[: len(parts)], out[len(parts) :]
 
 
@@ -126,11 +149,7 @@
     for g in range(owned):
         sums = []
         for p in range(len(parts)):
-            gross, *inbound = in_refs[p * each : (p + 1) * each]
-            total = gross[g]
-            for ref in inbound:
-                total += decode(ref[g])
-            sums.append(total)
+            sums.append(decode(*(ref[g] for ref in in_refs[p * each : (p + 1) * each])))
         gross = jnp.concatenate(sums, axis=0)
         ceded = jnp.minimum(jnp.maximum(gross - attach_ref[pl.ds(g, 1), :], 0.0), limit_ref[pl.ds(g, 1), :])
         ceded_ref[:, pl.ds(g * TB, TB)] = ceded
@@ -218,10 +237,7 @@
         if step < steps - 1:
             count //= 2
             for p in range(len(PARTS)):
-                total, *inbound = [a[count : 2 * count] for a in received[p]]
-                for a in inbound:
-                    total += decode(a)
-                sends[p] = encode(total)
+                sends[p] = add_coded(*(a[count : 2 * count] for a in received[p]))
     inbound = [a for arrays in received for a in arrays]
     ceded, pieces = retro(PARTS, inbound, attach, limit, share_values, other_shares, share_rblock)
     pieces = lax.all_to_all(pieces, "risk", split_axis=0, concat_axis=0, tiled=True)

time: 74.3 us -> 59.7 us (0.80)
  Pallas kernels: 22.9 us -> 8.64 us
    pallas_call x1, Pallas kernels: 19.8 us -> 5.47 us  [block_sums(): pl.pallas_call(functools.partial(block_sums_kernel, parts, owned, chunks)...]
where the time goes in v3:
time: 59.7 us; the launch traced here: 59.4 us
  waiting for transfers between devices  22.1 us (37%)
  blocking collectives  15.7 us (26%)
  starting transfers between devices  10.6 us (18%)
  Pallas kernels  8.64 us (14%)
  other arithmetic  1.6 us (3%)
  between operations  0.7 us (1%)
    ppermute x4, waiting for transfers between devices, dense_on_device(): received[p].append(lax.ppermute(sends[p], ('risk', 'tcol'), pairs))  22.1 us
    all_to_all x1, blocking collectives, dense_on_device(): lax.all_to_all(pieces, 'risk', split_axis=0, concat_axis=0, tiled=True)  15.7 us
    ppermute x4, starting transfers between devices, dense_on_device(): received[p].append(lax.ppermute(sends[p], ('risk', 'tcol'), pairs))  10.6 us
    pallas_call x1, Pallas kernels, block_sums(): pl.pallas_call(functools.partial(block_sums_kernel, parts, owned, chunks)...  5.47 us
    convert_element_type x3, other arithmetic, add_coded(): return jnp.minimum(steps, HALF - 1).astype(jnp.int16)  1.6 us
    pallas_call x1, Pallas kernels, finish(): pl.pallas_call(finish_kernel, out_shape=jax.ShapeDtypeStruct((RB // 4, 2...  1.59 us
    pallas_call x1, Pallas kernels, retro(): pl.pallas_call(functools.partial(retro_kernel, parts), grid=(1,), in_spec...  1.57 us
  transfers between devices with their start and end apart: 5, of which 4 were waited for; matrix products, arithmetic and copies ran while one was open for 0% of the time, Pallas kernels for 0%

profile of v3, /device:TPU:0, one launch (start us, length us, event | category | flops | bytes accessed | tf_op | source)
XLA Modules:
  0.0 59.4 jit_solution(6038424142325798295)
XLA Ops:
  0.6 5.5 %shard_map.140 = (s16[48,64,128]{2,1,0:T(8,128)(2,1)}, s16[48,64,128]{2,1,0:T(8,128)(2,1)}) custom-call(s32[64]{0:T(128)} %bitcast.15, s32[64]{0:T(128)} %refs_1_.1, bf16[64,64]{1,0:T(8,128)(2,1)} %refs_2_.1, f32[64,128]{1,0:T(8,128)} %bitcast.10, f32[64,128]{1,0:T(8,128)} %bitcast.11, f32[64,128]{1,0:T(8,128)} %bitcast.12, s32[64,128]{1,0:T(8,128)} %bitcast.13, ...), custom_call_target="tpu_custom_call" | custom-call | tf_op jit(solution)/shard_map/pallas_call | solution.py:124
  6.1 0.0 copy-start
  6.1 3.0 %collective-permute-start.1 = (s16[48,64,128]{2,1,0:T(8,128)(2,1)}, s16[48,64,128]{2,1,0:T(8,128)(2,1)S(1)}, u32[]{:S(2)}, u32[]{:S(2)}) collective-permute-start(s16[48,64,128]{2,1,0:T(8,128)(2,1)} %get-tuple-element.7), channel_id=1, source_target_pairs={{0,2},{1,5},{2,0},{3,7},{4,6},{5,1},{6,4},{7,3},{8,10},{9,13},{10,... | collective-permute-start | bytes 2359304 | tf_op jit(solution)/shard_map/ppermute | solution.py:236
  9.1 10.2 %collective-permute-done.1.refs_1_ = s16[48,64,128]{2,1,0:T(8,128)(2,1)S(1)} collective-permute-done((s16[48,64,128]{2,1,0:T(8,128)(2,1)}, s16[48,64,128]{2,1,0:T(8,128)(2,1)S(1)}, u32[]{:S(2)}, u32[]{:S(2)}) %collective-permute-start.1) | collective-permute-done | bytes 786464 | tf_op jit(solution)/shard_map/ppermute | solution.py:236
  19.3 1.3 %minimum_convert_fusion = s16[24,64,128]{2,1,0:T(8,128)(2,1)S(1)} fusion(s16[48,64,128]{2,1,0:T(8,128)(2,1)S(1)} %collective-permute-done.1.refs_1_, s16[48,64,128]{2,1,0:T(8,128)(2,1)} %get-tuple-element.6.refs_0_), kind=kLoop, calls=%fused_computation | loop fusion | flops 1179648 | bytes 1179648 | tf_op jit(solution)/shard_map/convert_element_type | solution.py:30
  20.6 0.0 copy-start.1
  20.6 2.1 %collective-permute-start.2 = (s16[24,64,128]{2,1,0:T(8,128)(2,1)S(1)}, s16[24,64,128]{2,1,0:T(8,128)(2,1)S(1)}, u32[]{:S(2)}, u32[]{:S(2)}) collective-permute-start(s16[24,64,128]{2,1,0:T(8,128)(2,1)S(1)} %minimum_convert_fusion), channel_id=1, source_target_pairs={{0,4},{1,3},{2,6},{3,1},{4,0},{5,7},{6,2},{7,5},{8,12},{9,11},{10,... | collective-permute-start | bytes 1179656 | tf_op jit(solution)/shard_map/ppermute | solution.py:236
  22.7 5.8 %collective-permute-done.2.refs_2_ = s16[24,64,128]{2,1,0:T(8,128)(2,1)S(1)} collective-permute-done((s16[24,64,128]{2,1,0:T(8,128)(2,1)S(1)}, s16[24,64,128]{2,1,0:T(8,128)(2,1)S(1)}, u32[]{:S(2)}, u32[]{:S(2)}) %collective-permute-start.2) | collective-permute-done | bytes 393248 | tf_op jit(solution)/shard_map/ppermute | solution.py:236
  28.5 0.0 copy-done
  28.5 0.2 minimum_convert_fusion.1
  28.7 0.0 copy-start.4
  28.7 2.1 %collective-permute-start.3 = (s16[12,64,128]{2,1,0:T(8,128)(2,1)S(1)}, s16[12,64,128]{2,1,0:T(8,128)(2,1)S(1)}, u32[]{:S(2)}, u32[]{:S(2)}) collective-permute-start(s16[12,64,128]{2,1,0:T(8,128)(2,1)S(1)} %minimum_convert_fusion.1), channel_id=1, source_target_pairs={{0,8},{1,9},{2,10},{3,11},{4,12},{5,13},{6,14},{7,15},{8,0},{9,1},... | collective-permute-start | bytes 589832 | tf_op jit(solution)/shard_map/ppermute | solution.py:236
  30.8 0.0 copy-done.1
  30.8 0.0 collective-permute-start
  30.8 3.6 %collective-permute-done.3.refs_3_ = s16[12,64,128]{2,1,0:T(8,128)(2,1)S(1)} collective-permute-done((s16[12,64,128]{2,1,0:T(8,128)(2,1)S(1)}, s16[12,64,128]{2,1,0:T(8,128)(2,1)S(1)}, u32[]{:S(2)}, u32[]{:S(2)}) %collective-permute-start.3) | collective-permute-done | bytes 196640 | tf_op jit(solution)/shard_map/ppermute | solution.py:236
  34.5 0.1 minimum_convert_fusion.2
  34.6 0.0 copy-start.2
  34.6 0.0 copy-start.3
  34.6 3.4 %collective-permute-start.4 = (s16[6,64,128]{2,1,0:T(8,128)(2,1)S(1)}, s16[6,64,128]{2,1,0:T(8,128)(2,1)S(1)}, u32[]{:S(2)}, u32[]{:S(2)}) collective-permute-start(s16[6,64,128]{2,1,0:T(8,128)(2,1)S(1)} %minimum_convert_fusion.2), channel_id=1, source_target_pairs={{0,16},{1,17},{2,18},{3,19},{4,20},{5,21},{6,22},{7,23},{8,24},{9,... | collective-permute-start | bytes 294920 | tf_op jit(solution)/shard_map/ppermute | solution.py:236
  38.0 0.0 copy-done.4
  38.0 0.1 copy.15.rblock_ref
  38.1 0.0 collective-permute-done.other_ref
  38.1 2.5 %collective-permute-done.4.refs_4_ = s16[6,64,128]{2,1,0:T(8,128)(2,1)S(1)} collective-permute-done((s16[6,64,128]{2,1,0:T(8,128)(2,1)S(1)}, s16[6,64,128]{2,1,0:T(8,128)(2,1)S(1)}, u32[]{:S(2)}, u32[]{:S(2)}) %collective-permute-start.4) | collective-permute-done | bytes 98336 | tf_op jit(solution)/shard_map/ppermute | solution.py:236
  40.6 0.0 copy-done.2
  40.6 0.0 copy-done.3
  40.6 1.6 %shard_map.141 = (f32[64,768]{1,0:T(8,128)}, f32[16,16,128]{2,1,0:T(8,128)S(1)}) custom-call(s32[6,2]{1,0:T(8,128)S(1)} %copy.15.rblock_ref, f32[6,128]{1,0:T(8,128)S(1)} %bitcast.8, f32[6,128]{1,0:T(8,128)S(1)} %bitcast.9, bf16[6,2,64,128]{3,2,1,0:T(8,128)(2,1)S(1)} %copy-done.1, bf16[6,2,64,128]{3,2,1,0:T(8,128)(2,1)S(1)} %collective-permute-done.other_ref, ...), custom_call_target="tpu_custom_call" | custom-call | tf_op jit(solution)/shard_map/pallas_call | solution.py:184
  42.2 15.7 %all_to_all.5.in_ref = f32[16,16,128]{2,1,0:T(8,128)} all-to-all(f32[16,16,128]{2,1,0:T(8,128)S(1)} %get-tuple-element.9), channel_id=1, replica_groups=mesh['risk'=16,'tcol'=2] {'risk'}, dimensions={0} | all-to-all | bytes 262144 | tf_op jit(solution)/shard_map/all_to_all | solution.py:243
  57.8 1.6 %shard_map.142 = f32[32,64]{1,0:T(8,128)} custom-call(f32[16,16,128]{2,1,0:T(8,128)} %all_to_all.5.in_ref), custom_call_target="tpu_custom_call" | custom-call | tf_op jit(solution)/shard_map/pallas_call | solution.py:207
Async XLA Ops:
  6.1 22.4 %copy-start = (s16[48,64,128]{2,1,0:T(8,128)(2,1)S(1)}, s16[48,64,128]{2,1,0:T(8,128)(2,1)}, u32[]{:S(2)}) copy-start(s16[48,64,128]{2,1,0:T(8,128)(2,1)} %get-tuple-element.6.refs_0_) | copy-start | bytes 2359300
  6.1 13.2 %collective-permute-start.1 = (s16[48,64,128]{2,1,0:T(8,128)(2,1)}, s16[48,64,128]{2,1,0:T(8,128)(2,1)S(1)}, u32[]{:S(2)}, u32[]{:S(2)}) collective-permute-start(s16[48,64,128]{2,1,0:T(8,128)(2,1)} %get-tuple-element.7), channel_id=1, source_target_pairs={{0,2},{1,5},{2,0},{3,7},{4,6},{5,1},{6,4},{7,3},{8,10},{9,13},{10,... | collective-permute-start | bytes 2359304 | tf_op jit(solution)/shard_map/ppermute | solution.py:236
  20.6 10.2 %copy-start.1 = (bf16[6,2,64,128]{3,2,1,0:T(8,128)(2,1)S(1)}, bf16[6,2,64,128]{3,2,1,0:T(8,128)(2,1)}, u32[]{:S(2)}) copy-start(bf16[6,2,64,128]{3,2,1,0:T(8,128)(2,1)} %mine_ref.1) | copy-start | bytes 589828
  20.6 7.9 %collective-permute-start.2 = (s16[24,64,128]{2,1,0:T(8,128)(2,1)S(1)}, s16[24,64,128]{2,1,0:T(8,128)(2,1)S(1)}, u32[]{:S(2)}, u32[]{:S(2)}) collective-permute-start(s16[24,64,128]{2,1,0:T(8,128)(2,1)S(1)} %minimum_convert_fusion), channel_id=1, source_target_pairs={{0,4},{1,3},{2,6},{3,1},{4,0},{5,7},{6,2},{7,5},{8,12},{9,11},{10,... | collective-permute-start | bytes 1179656 | tf_op jit(solution)/shard_map/ppermute | solution.py:236
  28.7 9.3 %copy-start.4 = (s32[6,2]{0,1:T(2,128)S(1)}, s32[6,2]{0,1:T(2,128)}, u32[]{:S(2)}) copy-start(s32[6,2]{0,1:T(2,128)} %param.25) | copy-start | bytes 148
  28.7 5.8 %collective-permute-start.3 = (s16[12,64,128]{2,1,0:T(8,128)(2,1)S(1)}, s16[12,64,128]{2,1,0:T(8,128)(2,1)S(1)}, u32[]{:S(2)}, u32[]{:S(2)}) collective-permute-start(s16[12,64,128]{2,1,0:T(8,128)(2,1)S(1)} %minimum_convert_fusion.1), channel_id=1, source_target_pairs={{0,8},{1,9},{2,10},{3,11},{4,12},{5,13},{6,14},{7,15},{8,0},{9,1},... | collective-permute-start | bytes 589832 | tf_op jit(solution)/shard_map/ppermute | solution.py:236
  30.8 7.3 %collective-permute-start = (bf16[6,2,64,128]{3,2,1,0:T(8,128)(2,1)S(1)}, bf16[6,2,64,128]{3,2,1,0:T(8,128)(2,1)S(1)}, u32[]{:S(2)}, u32[]{:S(2)}) collective-permute-start(bf16[6,2,64,128]{3,2,1,0:T(8,128)(2,1)S(1)} %copy-done.1), channel_id=1, source_target_pairs={{0,1},{1,0},{2,3},{3,2},{4,5},{5,4},{6,7},{7,6},{8,9},{9,8},{10,11... | collective-permute-start | bytes 589832 | tf_op jit(solution)/shard_map/ppermute | solution.py:222
  34.6 6.0 %copy-start.2 = (f32[768]{0:T(1024)S(1)}, f32[768]{0:T(1024)}, u32[]{:S(2)}) copy-start(f32[768]{0:T(1024)} %param.22) | copy-start | bytes 9220
  34.6 6.0 %copy-start.3 = (f32[768]{0:T(1024)S(1)}, f32[768]{0:T(1024)}, u32[]{:S(2)}) copy-start(f32[768]{0:T(1024)} %param.23) | copy-start | bytes 9220
  34.6 5.9 %collective-permute-start.4 = (s16[6,64,128]{2,1,0:T(8,128)(2,1)S(1)}, s16[6,64,128]{2,1,0:T(8,128)(2,1)S(1)}, u32[]{:S(2)}, u32[]{:S(2)}) collective-permute-start(s16[6,64,128]{2,1,0:T(8,128)(2,1)S(1)} %minimum_convert_fusion.2), channel_id=1, source_target_pairs={{0,16},{1,17},{2,18},{3,19},{4,20},{5,21},{6,22},{7,23},{8,24},{9,... | collective-permute-start | bytes 294920 | tf_op jit(solution)/shard_map/ppermute | solution.py:236

commit v4 on v3

--- a/solution.py
+++ b/solution.py
@@ -194,23 +194,12 @@
     )(rblock, attach, limit, mine, other, *inbound)
 
 
-def finish_kernel(in_ref, out_ref):
-    total = in_ref[0]
-    for s in range(1, in_ref.shape[0]):
-        total += in_ref[s]
-    half, years = out_ref.shape[0] // 2, out_ref.shape[1]
-    for h in range(2):
-        out_ref[pl.ds(h * half, half), :] = total[:, h * years : (h + 1) * years]
-
-
 def finish(pieces):
-    return pl.pallas_call(
-        finish_kernel,
-        out_shape=jax.ShapeDtypeStruct((RB // 4, 2 * RB // 4), jnp.float32),
-    )(pieces).T
-
-
-PARTS = ((0, 64, ((0, 1, 2, 3), (1, 0, 2, 3))),)
+    years = pieces.shape[2] // 2
+    return jnp.concatenate([jnp.sum(pieces[:, :, h * years : (h + 1) * years], axis=0) for h in range(2)], axis=0).T
+
+
+PARTS = ((0, 16, ((0, 1, 2, 3), (1, 0, 2, 3))), (16, 16, ((0, 1, 2, 3), (1, 0, 2, 3))), (32, 16, ((0, 1, 2, 3), (1, 0, 2, 3))), (48, 16, ((2, 3, 0, 1), (2, 3, 1, 0))),)
 
 
 def dense_on_device(

time: 59.7 us -> 52.9 us (0.89)
  waiting for transfers between devices: 22.1 us -> 4.54 us
  starting transfers between devices: 10.6 us -> 25.7 us
  blocking collectives: 15.7 us -> 12 us
  Pallas kernels: 8.64 us -> 7.19 us
  other arithmetic: 1.6 us -> 2.27 us
    ppermute x4 -> x16, waiting for transfers between devices: 22.1 us -> 4.53 us  [dense_on_device(): received[p].append(lax.ppermute(sends[p], ('risk', 'tcol'), pairs))]
    ppermute x4 -> x16, starting transfers between devices: 10.6 us -> 25.7 us  [dense_on_device(): received[p].append(lax.ppermute(sends[p], ('risk', 'tcol'), pairs))]
    all_to_all x1, blocking collectives: 15.7 us -> 12 us  [dense_on_device(): lax.all_to_all(pieces, 'risk', split_axis=0, concat_axis=0, tiled=True)]
    pallas_call x1 -> x0, Pallas kernels: 1.59 us -> none  [finish(): pl.pallas_call(finish_kernel, out_shape=jax.ShapeDtypeStruct((RB // 4, 2...]
    transpose x0 -> x1, other arithmetic: none -> 0.61 us  [finish(): jnp.concatenate([jnp.sum(pieces[:, :, h * years:(h + 1) * years], axis=0)...]
    convert_element_type x3 -> x12, other arithmetic: 1.6 us -> 1.56 us  [add_coded(): return jnp.minimum(steps, HALF - 1).astype(jnp.int16)]
  transfers between devices with their start and end apart: 5 -> 17, of which waited for: 4 -> 5; matrix products, arithmetic and copies ran while one was open for 0% -> 3% of each run, Pallas kernels for 0% -> 0%
where the time goes in v4:
time: 52.9 us; the launch traced here: 52.6 us
  starting transfers between devices  25.7 us (49%)
  blocking collectives  12 us (23%)
  Pallas kernels  7.19 us (14%)
  waiting for transfers between devices  4.54 us (9%)
  other arithmetic  2.27 us (4%)
  between operations  0.78 us (1%)
    ppermute x16, starting transfers between devices, dense_on_device(): received[p].append(lax.ppermute(sends[p], ('risk', 'tcol'), pairs))  25.7 us
    all_to_all x1, blocking collectives, dense_on_device(): lax.all_to_all(pieces, 'risk', split_axis=0, concat_axis=0, tiled=True)  12 us
    pallas_call x1, Pallas kernels, block_sums(): pl.pallas_call(functools.partial(block_sums_kernel, parts, owned, chunks)...  5.62 us
    ppermute x16, waiting for transfers between devices, dense_on_device(): received[p].append(lax.ppermute(sends[p], ('risk', 'tcol'), pairs))  4.53 us
    pallas_call x1, Pallas kernels, retro(): pl.pallas_call(functools.partial(retro_kernel, parts), grid=(1,), in_spec...  1.57 us
    convert_element_type x12, other arithmetic, add_coded(): return jnp.minimum(steps, HALF - 1).astype(jnp.int16)  1.56 us
  transfers between devices with their start and end apart: 17, of which 5 were waited for; matrix products, arithmetic and copies ran while one was open for 3% of the time, Pallas kernels for 0%

profile of v4, /device:TPU:0, one launch (start us, length us, event | category | flops | bytes accessed | tf_op | source)
XLA Modules:
  0.0 52.6 jit_solution(9133448261536740961)
XLA Ops:
  0.6 0.0 copy-start.4
  0.6 5.6 %shard_map.140 = (s16[48,16,128]{2,1,0:T(8,128)(2,1)}, s16[48,16,128]{2,1,0:T(8,128)(2,1)}, s16[48,16,128]{2,1,0:T(8,128)(2,1)}, s16[48,16,128]{2,1,0:T(8,128)(2...) custom-call(s32[64]{0:T(128)} %bitcast.15, ...), custom_call_target="tpu_custom_call" | custom-call | tf_op jit(solution)/shard_map/pallas_call | solution.py:124
  6.3 0.0 copy-start.1
  6.3 3.0 %collective-permute-start.1 = (s16[48,16,128]{2,1,0:T(8,128)(2,1)}, s16[48,16,128]{2,1,0:T(8,128)(2,1)S(1)}, u32[]{:S(2)}, u32[]{:S(2)}) collective-permute-start(s16[48,16,128]{2,1,0:T(8,128)(2,1)} %get-tuple-element.13), channel_id=1, source_target_pairs={{0,2},{1,5},{2,0},{3,7},{4,6},{5,1},{6,4},{7,3},{8,10},{9,13},{10,... | collective-permute-start | bytes 589832 | tf_op jit(solution)/shard_map/ppermute | solution.py:225
  9.3 0.0 copy-done.4
  9.3 0.0 collective-permute-start
  9.3 1.1 %collective-permute-start.5 = (s16[48,16,128]{2,1,0:T(8,128)(2,1)}, s16[48,16,128]{2,1,0:T(8,128)(2,1)S(1)}, u32[]{:S(2)}, u32[]{:S(2)}) collective-permute-start(s16[48,16,128]{2,1,0:T(8,128)(2,1)} %get-tuple-element.15), channel_id=1, source_target_pairs={{0,2},{1,5},{2,0},{3,7},{4,6},{5,1},{6,4},{7,3},{8,10},{9,13},{10,... | collective-permute-start | bytes 589832 | tf_op jit(solution)/shard_map/ppermute | solution.py:225
  10.4 1.0 %collective-permute-start.9 = (s16[48,16,128]{2,1,0:T(8,128)(2,1)}, s16[48,16,128]{2,1,0:T(8,128)(2,1)S(1)}, u32[]{:S(2)}, u32[]{:S(2)}) collective-permute-start(s16[48,16,128]{2,1,0:T(8,128)(2,1)} %get-tuple-element.17), channel_id=1, source_target_pairs={{0,2},{1,5},{2,0},{3,7},{4,6},{5,1},{6,4},{7,3},{8,10},{9,13},{10,... | collective-permute-start | bytes 589832 | tf_op jit(solution)/shard_map/ppermute | solution.py:225
  11.3 1.6 %collective-permute-start.13 = (s16[48,16,128]{2,1,0:T(8,128)(2,1)}, s16[48,16,128]{2,1,0:T(8,128)(2,1)S(1)}, u32[]{:S(2)}, u32[]{:S(2)}) collective-permute-start(s16[48,16,128]{2,1,0:T(8,128)(2,1)} %get-tuple-element.19), channel_id=1, source_target_pairs={{0,8},{1,9},{2,10},{3,11},{4,12},{5,13},{6,14},{7,15},{8,0},{9,1},... | collective-permute-start | bytes 589832 | tf_op jit(solution)/shard_map/ppermute | solution.py:225
  12.9 0.3 collective-permute-done.1.refs_1_
  13.2 1.0 %minimum_convert_fusion.3 = s16[24,16,128]{2,1,0:T(8,128)(2,1)S(1)} fusion(s16[48,16,128]{2,1,0:T(8,128)(2,1)S(1)} %collective-permute-done.1.refs_1_, s16[48,16,128]{2,1,0:T(8,128)(2,1)} %get-tuple-element.12.refs_0_), kind=kLoop, calls=%fused_computation.3 | loop fusion | flops 294912 | bytes 294912 | tf_op jit(solution)/shard_map/convert_element_type | solution.py:30
  14.1 0.0 copy-start.2
  14.1 2.1 %collective-permute-start.2 = (s16[24,16,128]{2,1,0:T(8,128)(2,1)S(1)}, s16[24,16,128]{2,1,0:T(8,128)(2,1)S(1)}, u32[]{:S(2)}, u32[]{:S(2)}) collective-permute-start(s16[24,16,128]{2,1,0:T(8,128)(2,1)S(1)} %minimum_convert_fusion.3), channel_id=1, source_target_pairs={{0,4},{1,3},{2,6},{3,1},{4,0},{5,7},{6,2},{7,5},{8,12},{9,11},{10,... | collective-permute-start | bytes 294920 | tf_op jit(solution)/shard_map/ppermute | solution.py:225
  16.2 0.0 collective-permute-done.5.refs_6_
  16.2 0.0 copy-done.1
  16.3 0.1 minimum_convert_fusion.2
  16.3 0.0 copy-start.3
  16.3 1.1 %collective-permute-start.6 = (s16[24,16,128]{2,1,0:T(8,128)(2,1)S(1)}, s16[24,16,128]{2,1,0:T(8,128)(2,1)S(1)}, u32[]{:S(2)}, u32[]{:S(2)}) collective-permute-start(s16[24,16,128]{2,1,0:T(8,128)(2,1)S(1)} %minimum_convert_fusion.2), channel_id=1, source_target_pairs={{0,4},{1,3},{2,6},{3,1},{4,0},{5,7},{6,2},{7,5},{8,12},{9,11},{10,... | collective-permute-start | bytes 294920 | tf_op jit(solution)/shard_map/ppermute | solution.py:225
  17.5 1.1 %collective-permute-done.9.refs_11_ = s16[48,16,128]{2,1,0:T(8,128)(2,1)S(1)} collective-permute-done((s16[48,16,128]{2,1,0:T(8,128)(2,1)}, s16[48,16,128]{2,1,0:T(8,128)(2,1)S(1)}, u32[]{:S(2)}, u32[]{:S(2)}) %collective-permute-start.9) | collective-permute-done | bytes 196640 | tf_op jit(solution)/shard_map/ppermute | solution.py:225
  18.5 0.0 copy-done.2
  18.5 0.1 minimum_convert_fusion.1
  18.6 0.0 copy-start
  18.6 2.5 %collective-permute-start.10 = (s16[24,16,128]{2,1,0:T(8,128)(2,1)S(1)}, s16[24,16,128]{2,1,0:T(8,128)(2,1)S(1)}, u32[]{:S(2)}, u32[]{:S(2)}) collective-permute-start(s16[24,16,128]{2,1,0:T(8,128)(2,1)S(1)} %minimum_convert_fusion.1), channel_id=1, source_target_pairs={{0,4},{1,3},{2,6},{3,1},{4,0},{5,7},{6,2},{7,5},{8,12},{9,11},{10,... | collective-permute-start | bytes 294920 | tf_op jit(solution)/shard_map/ppermute | solution.py:225
  21.1 0.0 collective-permute-done.13.refs_16_
  21.1 0.0 copy-done.3
  21.1 0.1 minimum_convert_fusion
  21.2 2.7 %collective-permute-start.14 = (s16[24,16,128]{2,1,0:T(8,128)(2,1)S(1)}, s16[24,16,128]{2,1,0:T(8,128)(2,1)S(1)}, u32[]{:S(2)}, u32[]{:S(2)}) collective-permute-start(s16[24,16,128]{2,1,0:T(8,128)(2,1)S(1)} %minimum_convert_fusion), channel_id=1, source_target_pairs={{0,16},{1,17},{2,18},{3,19},{4,20},{5,21},{6,22},{7,23},{8,24},{9,... | collective-permute-start | bytes 294920 | tf_op jit(solution)/shard_map/ppermute | solution.py:225
  23.8 0.0 collective-permute-done.2.refs_2_
  23.8 0.0 copy-done
  23.8 0.1 minimum_convert_fusion.7
  23.9 1.6 %collective-permute-start.3 = (s16[12,16,128]{2,1,0:T(8,128)(2,1)S(1)}, s16[12,16,128]{2,1,0:T(8,128)(2,1)S(1)}, u32[]{:S(2)}, u32[]{:S(2)}) collective-permute-start(s16[12,16,128]{2,1,0:T(8,128)(2,1)S(1)} %minimum_convert_fusion.7), channel_id=1, source_target_pairs={{0,8},{1,9},{2,10},{3,11},{4,12},{5,13},{6,14},{7,15},{8,0},{9,1},... | collective-permute-start | bytes 147464 | tf_op jit(solution)/shard_map/ppermute | solution.py:225
  25.5 0.0 collective-permute-done.6.refs_7_
  25.5 0.1 minimum_convert_fusion.6
  25.6 0.5 %collective-permute-start.7 = (s16[12,16,128]{2,1,0:T(8,128)(2,1)S(1)}, s16[12,16,128]{2,1,0:T(8,128)(2,1)S(1)}, u32[]{:S(2)}, u32[]{:S(2)}) collective-permute-start(s16[12,16,128]{2,1,0:T(8,128)(2,1)S(1)} %minimum_convert_fusion.6), channel_id=1, source_target_pairs={{0,8},{1,9},{2,10},{3,11},{4,12},{5,13},{6,14},{7,15},{8,0},{9,1},... | collective-permute-start | bytes 147464 | tf_op jit(solution)/shard_map/ppermute | solution.py:225
  26.1 0.0 collective-permute-done.10.refs_12_
  26.1 0.1 minimum_convert_fusion.5
  26.2 1.6 %collective-permute-start.11 = (s16[12,16,128]{2,1,0:T(8,128)(2,1)S(1)}, s16[12,16,128]{2,1,0:T(8,128)(2,1)S(1)}, u32[]{:S(2)}, u32[]{:S(2)}) collective-permute-start(s16[12,16,128]{2,1,0:T(8,128)(2,1)S(1)} %minimum_convert_fusion.5), channel_id=1, source_target_pairs={{0,8},{1,9},{2,10},{3,11},{4,12},{5,13},{6,14},{7,15},{8,0},{9,1},... | collective-permute-start | bytes 147464 | tf_op jit(solution)/shard_map/ppermute | solution.py:225
  27.8 0.0 collective-permute-done.14.refs_17_
  27.8 0.1 minimum_convert_fusion.4
  27.9 1.6 %collective-permute-start.15 = (s16[12,16,128]{2,1,0:T(8,128)(2,1)S(1)}, s16[12,16,128]{2,1,0:T(8,128)(2,1)S(1)}, u32[]{:S(2)}, u32[]{:S(2)}) collective-permute-start(s16[12,16,128]{2,1,0:T(8,128)(2,1)S(1)} %minimum_convert_fusion.4), channel_id=1, source_target_pairs={{0,2},{1,5},{2,0},{3,7},{4,6},{5,1},{6,4},{7,3},{8,10},{9,13},{10,... | collective-permute-start | bytes 147464 | tf_op jit(solution)/shard_map/ppermute | solution.py:225
  29.4 0.0 collective-permute-done.3.refs_3_
  29.5 1.7 %collective-permute-start.4 = (s16[6,16,128]{2,1,0:T(8,128)(2,1)S(1)}, s16[6,16,128]{2,1,0:T(8,128)(2,1)S(1)}, u32[]{:S(2)}, u32[]{:S(2)}) collective-permute-start(s16[6,16,128]{2,1,0:T(8,128)(2,1)S(1)} %minimum_convert_fusion.11), channel_id=1, source_target_pairs={{0,16},{1,17},{2,18},{3,19},{4,20},{5,21},{6,22},{7,23},{8,24},{9,... | collective-permute-start | bytes 73736 | tf_op jit(solution)/shard_map/ppermute | solution.py:225
  31.2 0.0 collective-permute-done.7.refs_8_
  31.2 1.4 %collective-permute-start.8 = (s16[6,16,128]{2,1,0:T(8,128)(2,1)S(1)}, s16[6,16,128]{2,1,0:T(8,128)(2,1)S(1)}, u32[]{:S(2)}, u32[]{:S(2)}) collective-permute-start(s16[6,16,128]{2,1,0:T(8,128)(2,1)S(1)} %minimum_convert_fusion.10), channel_id=1, source_target_pairs={{0,16},{1,17},{2,18},{3,19},{4,20},{5,21},{6,22},{7,23},{8,24},{9,... | collective-permute-start | bytes 73736 | tf_op jit(solution)/shard_map/ppermute | solution.py:225
  32.6 0.0 collective-permute-done.11.refs_13_
  32.6 0.0 copy-start.7
  32.6 1.7 %collective-permute-start.12 = (s16[6,16,128]{2,1,0:T(8,128)(2,1)S(1)}, s16[6,16,128]{2,1,0:T(8,128)(2,1)S(1)}, u32[]{:S(2)}, u32[]{:S(2)}) collective-permute-start(s16[6,16,128]{2,1,0:T(8,128)(2,1)S(1)} %minimum_convert_fusion.9), channel_id=1, source_target_pairs={{0,16},{1,17},{2,18},{3,19},{4,20},{5,21},{6,22},{7,23},{8,24},{9,... | collective-permute-start | bytes 73736 | tf_op jit(solution)/shard_map/ppermute | solution.py:225
  34.3 0.0 collective-permute-done.15.refs_18_
  34.4 0.0 copy-start.5
  34.4 0.0 copy-start.6
  34.4 0.6 %collective-permute-start.16 = (s16[6,16,128]{2,1,0:T(8,128)(2,1)S(1)}, s16[6,16,128]{2,1,0:T(8,128)(2,1)S(1)}, u32[]{:S(2)}, u32[]{:S(2)}) collective-permute-start(s16[6,16,128]{2,1,0:T(8,128)(2,1)S(1)} %minimum_convert_fusion.8), channel_id=1, source_target_pairs={{0,4},{1,3},{2,6},{3,1},{4,0},{5,7},{6,2},{7,5},{8,12},{9,11},{10,... | collective-permute-start | bytes 73736 | tf_op jit(solution)/shard_map/ppermute | solution.py:225
  35.0 0.0 copy-done.7
  35.0 0.1 copy.15.rblock_ref
  35.1 0.0 collective-permute-done.other_ref
  35.1 0.0 collective-permute-done.4.refs_4_
  35.1 0.9 %collective-permute-done.8.refs_9_ = s16[6,16,128]{2,1,0:T(8,128)(2,1)S(1)} collective-permute-done((s16[6,16,128]{2,1,0:T(8,128)(2,1)S(1)}, s16[6,16,128]{2,1,0:T(8,128)(2,1)S(1)}, u32[]{:S(2)}, u32[]{:S(2)}) %collective-permute-start.8) | collective-permute-done | bytes 24608 | tf_op jit(solution)/shard_map/ppermute | solution.py:225
  36.0 1.4 %collective-permute-done.12.refs_14_ = s16[6,16,128]{2,1,0:T(8,128)(2,1)S(1)} collective-permute-done((s16[6,16,128]{2,1,0:T(8,128)(2,1)S(1)}, s16[6,16,128]{2,1,0:T(8,128)(2,1)S(1)}, u32[]{:S(2)}, u32[]{:S(2)}) %collective-permute-start.12) | collective-permute-done | bytes 24608 | tf_op jit(solution)/shard_map/ppermute | solution.py:225
  37.4 0.9 %collective-permute-done.16.refs_19_ = s16[6,16,128]{2,1,0:T(8,128)(2,1)S(1)} collective-permute-done((s16[6,16,128]{2,1,0:T(8,128)(2,1)S(1)}, s16[6,16,128]{2,1,0:T(8,128)(2,1)S(1)}, u32[]{:S(2)}, u32[]{:S(2)}) %collective-permute-start.16) | collective-permute-done | bytes 24608 | tf_op jit(solution)/shard_map/ppermute | solution.py:225
  38.3 0.0 copy-done.5
  38.3 0.0 copy-done.6
  38.3 1.6 %shard_map.141 = (f32[64,768]{1,0:T(8,128)}, f32[16,16,128]{2,1,0:T(8,128)S(1)}) custom-call(s32[6,2]{1,0:T(8,128)S(1)} %copy.15.rblock_ref, f32[6,128]{1,0:T(8,128)S(1)} %bitcast.9, f32[6,128]{1,0:T(8,128)S(1)} %bitcast.10, bf16[6,2,64,128]{3,2,1,0:T(8,128)(2,1)S(1)} %copy-done.4, bf16[6,2,64,128]{3,2,1,0:T(8,128)(2,1)S(1)} %collective-permute-done.other_ref, ...), custom_call_target="tpu_custom_call" | custom-call | tf_op jit(solution)/shard_map/pallas_call | solution.py:184
  39.9 12.0 %all_to_all.5 = f32[16,16,128]{2,1,0:T(8,128)S(1)} all-to-all(f32[16,16,128]{2,1,0:T(8,128)S(1)} %get-tuple-element.21), channel_id=1, replica_groups=mesh['risk'=16,'tcol'=2] {'risk'}, dimensions={0} | all-to-all | bytes 262144 | tf_op jit(solution)/shard_map/all_to_all | solution.py:232
  51.9 0.1 slice_reduce_fusion.1
  52.0 0.6 %maximum_bitcast_fusion = f32[64,32]{0,1:T(8,128)} fusion(f32[16,64]{1,0:T(8,128)S(1)} %get-tuple-element.23, f32[16,64]{1,0:T(8,128)S(1)} %get-tuple-element.22), kind=kLoop, calls=%fused_computation.14 | loop fusion | flops 2048 | bytes 16384 | tf_op jit(solution)/shard_map/transpose | solution.py:199
  (4 shorter events, 0.1 us)
Async XLA Ops:
  0.6 8.7 %copy-start.4 = (bf16[6,2,64,128]{3,2,1,0:T(8,128)(2,1)S(1)}, bf16[6,2,64,128]{3,2,1,0:T(8,128)(2,1)}, u32[]{:S(2)}) copy-start(bf16[6,2,64,128]{3,2,1,0:T(8,128)(2,1)} %mine_ref.1) | copy-start | bytes 589828
  6.3 10.0 %copy-start.1 = (s16[48,16,128]{2,1,0:T(8,128)(2,1)S(1)}, s16[48,16,128]{2,1,0:T(8,128)(2,1)}, u32[]{:S(2)}) copy-start(s16[48,16,128]{2,1,0:T(8,128)(2,1)} %get-tuple-element.14.refs_5_) | copy-start | bytes 589828
  6.3 6.9 %collective-permute-start.1 = (s16[48,16,128]{2,1,0:T(8,128)(2,1)}, s16[48,16,128]{2,1,0:T(8,128)(2,1)S(1)}, u32[]{:S(2)}, u32[]{:S(2)}) collective-permute-start(s16[48,16,128]{2,1,0:T(8,128)(2,1)} %get-tuple-element.13), channel_id=1, source_target_pairs={{0,2},{1,5},{2,0},{3,7},{4,6},{5,1},{6,4},{7,3},{8,10},{9,13},{10,... | collective-permute-start | bytes 589832 | tf_op jit(solution)/shard_map/ppermute | solution.py:225
  9.3 25.8 %collective-permute-start = (bf16[6,2,64,128]{3,2,1,0:T(8,128)(2,1)S(1)}, bf16[6,2,64,128]{3,2,1,0:T(8,128)(2,1)S(1)}, u32[]{:S(2)}, u32[]{:S(2)}) collective-permute-start(bf16[6,2,64,128]{3,2,1,0:T(8,128)(2,1)S(1)} %copy-done.4), channel_id=1, source_target_pairs={{0,1},{1,0},{2,3},{3,2},{4,5},{5,4},{6,7},{7,6},{8,9},{9,8},{10,11... | collective-permute-start | bytes 589832 | tf_op jit(solution)/shard_map/ppermute | solution.py:211
  9.3 7.0 %collective-permute-start.5 = (s16[48,16,128]{2,1,0:T(8,128)(2,1)}, s16[48,16,128]{2,1,0:T(8,128)(2,1)S(1)}, u32[]{:S(2)}, u32[]{:S(2)}) collective-permute-start(s16[48,16,128]{2,1,0:T(8,128)(2,1)} %get-tuple-element.15), channel_id=1, source_target_pairs={{0,2},{1,5},{2,0},{3,7},{4,6},{5,1},{6,4},{7,3},{8,10},{9,13},{10,... | collective-permute-start | bytes 589832 | tf_op jit(solution)/shard_map/ppermute | solution.py:225
  10.4 8.2 %collective-permute-start.9 = (s16[48,16,128]{2,1,0:T(8,128)(2,1)}, s16[48,16,128]{2,1,0:T(8,128)(2,1)S(1)}, u32[]{:S(2)}, u32[]{:S(2)}) collective-permute-start(s16[48,16,128]{2,1,0:T(8,128)(2,1)} %get-tuple-element.17), channel_id=1, source_target_pairs={{0,2},{1,5},{2,0},{3,7},{4,6},{5,1},{6,4},{7,3},{8,10},{9,13},{10,... | collective-permute-start | bytes 589832 | tf_op jit(solution)/shard_map/ppermute | solution.py:225
  11.3 9.8 %collective-permute-start.13 = (s16[48,16,128]{2,1,0:T(8,128)(2,1)}, s16[48,16,128]{2,1,0:T(8,128)(2,1)S(1)}, u32[]{:S(2)}, u32[]{:S(2)}) collective-permute-start(s16[48,16,128]{2,1,0:T(8,128)(2,1)} %get-tuple-element.19), channel_id=1, source_target_pairs={{0,8},{1,9},{2,10},{3,11},{4,12},{5,13},{6,14},{7,15},{8,0},{9,1},... | collective-permute-start | bytes 589832 | tf_op jit(solution)/shard_map/ppermute | solution.py:225
  14.1 4.4 %copy-start.2 = (s16[48,16,128]{2,1,0:T(8,128)(2,1)S(1)}, s16[48,16,128]{2,1,0:T(8,128)(2,1)}, u32[]{:S(2)}) copy-start(s16[48,16,128]{2,1,0:T(8,128)(2,1)} %get-tuple-element.16.refs_10_) | copy-start | bytes 589828
  14.1 9.7 %collective-permute-start.2 = (s16[24,16,128]{2,1,0:T(8,128)(2,1)S(1)}, s16[24,16,128]{2,1,0:T(8,128)(2,1)S(1)}, u32[]{:S(2)}, u32[]{:S(2)}) collective-permute-start(s16[24,16,128]{2,1,0:T(8,128)(2,1)S(1)} %minimum_convert_fusion.3), channel_id=1, source_target_pairs={{0,4},{1,3},{2,6},{3,1},{4,0},{5,7},{6,2},{7,5},{8,12},{9,11},{10,... | collective-permute-start | bytes 294920 | tf_op jit(solution)/shard_map/ppermute | solution.py:225
  16.3 4.8 %copy-start.3 = (s16[48,16,128]{2,1,0:T(8,128)(2,1)S(1)}, s16[48,16,128]{2,1,0:T(8,128)(2,1)}, u32[]{:S(2)}) copy-start(s16[48,16,128]{2,1,0:T(8,128)(2,1)} %get-tuple-element.18.refs_15_) | copy-start | bytes 589828
  16.3 9.2 %collective-permute-start.6 = (s16[24,16,128]{2,1,0:T(8,128)(2,1)S(1)}, s16[24,16,128]{2,1,0:T(8,128)(2,1)S(1)}, u32[]{:S(2)}, u32[]{:S(2)}) collective-permute-start(s16[24,16,128]{2,1,0:T(8,128)(2,1)S(1)} %minimum_convert_fusion.2), channel_id=1, source_target_pairs={{0,4},{1,3},{2,6},{3,1},{4,0},{5,7},{6,2},{7,5},{8,12},{9,11},{10,... | collective-permute-start | bytes 294920 | tf_op jit(solution)/shard_map/ppermute | solution.py:225
  18.6 5.2 %copy-start = (s16[48,16,128]{2,1,0:T(8,128)(2,1)S(1)}, s16[48,16,128]{2,1,0:T(8,128)(2,1)}, u32[]{:S(2)}) copy-start(s16[48,16,128]{2,1,0:T(8,128)(2,1)} %get-tuple-element.12.refs_0_) | copy-start | bytes 589828
  18.6 7.5 %collective-permute-start.10 = (s16[24,16,128]{2,1,0:T(8,128)(2,1)S(1)}, s16[24,16,128]{2,1,0:T(8,128)(2,1)S(1)}, u32[]{:S(2)}, u32[]{:S(2)}) collective-permute-start(s16[24,16,128]{2,1,0:T(8,128)(2,1)S(1)} %minimum_convert_fusion.1), channel_id=1, source_target_pairs={{0,4},{1,3},{2,6},{3,1},{4,0},{5,7},{6,2},{7,5},{8,12},{9,11},{10,... | collective-permute-start | bytes 294920 | tf_op jit(solution)/shard_map/ppermute | solution.py:225
  21.2 6.6 %collective-permute-start.14 = (s16[24,16,128]{2,1,0:T(8,128)(2,1)S(1)}, s16[24,16,128]{2,1,0:T(8,128)(2,1)S(1)}, u32[]{:S(2)}, u32[]{:S(2)}) collective-permute-start(s16[24,16,128]{2,1,0:T(8,128)(2,1)S(1)} %minimum_convert_fusion), channel_id=1, source_target_pairs={{0,16},{1,17},{2,18},{3,19},{4,20},{5,21},{6,22},{7,23},{8,24},{9,... | collective-permute-start | bytes 294920 | tf_op jit(solution)/shard_map/ppermute | solution.py:225
  23.9 5.5 %collective-permute-start.3 = (s16[12,16,128]{2,1,0:T(8,128)(2,1)S(1)}, s16[12,16,128]{2,1,0:T(8,128)(2,1)S(1)}, u32[]{:S(2)}, u32[]{:S(2)}) collective-permute-start(s16[12,16,128]{2,1,0:T(8,128)(2,1)S(1)} %minimum_convert_fusion.7), channel_id=1, source_target_pairs={{0,8},{1,9},{2,10},{3,11},{4,12},{5,13},{6,14},{7,15},{8,0},{9,1},... | collective-permute-start | bytes 147464 | tf_op jit(solution)/shard_map/ppermute | solution.py:225
  25.6 5.6 %collective-permute-start.7 = (s16[12,16,128]{2,1,0:T(8,128)(2,1)S(1)}, s16[12,16,128]{2,1,0:T(8,128)(2,1)S(1)}, u32[]{:S(2)}, u32[]{:S(2)}) collective-permute-start(s16[12,16,128]{2,1,0:T(8,128)(2,1)S(1)} %minimum_convert_fusion.6), channel_id=1, source_target_pairs={{0,8},{1,9},{2,10},{3,11},{4,12},{5,13},{6,14},{7,15},{8,0},{9,1},... | collective-permute-start | bytes 147464 | tf_op jit(solution)/shard_map/ppermute | solution.py:225
  26.2 6.4 %collective-permute-start.11 = (s16[12,16,128]{2,1,0:T(8,128)(2,1)S(1)}, s16[12,16,128]{2,1,0:T(8,128)(2,1)S(1)}, u32[]{:S(2)}, u32[]{:S(2)}) collective-permute-start(s16[12,16,128]{2,1,0:T(8,128)(2,1)S(1)} %minimum_convert_fusion.5), channel_id=1, source_target_pairs={{0,8},{1,9},{2,10},{3,11},{4,12},{5,13},{6,14},{7,15},{8,0},{9,1},... | collective-permute-start | bytes 147464 | tf_op jit(solution)/shard_map/ppermute | solution.py:225
  27.9 6.5 %collective-permute-start.15 = (s16[12,16,128]{2,1,0:T(8,128)(2,1)S(1)}, s16[12,16,128]{2,1,0:T(8,128)(2,1)S(1)}, u32[]{:S(2)}, u32[]{:S(2)}) collective-permute-start(s16[12,16,128]{2,1,0:T(8,128)(2,1)S(1)} %minimum_convert_fusion.4), channel_id=1, source_target_pairs={{0,2},{1,5},{2,0},{3,7},{4,6},{5,1},{6,4},{7,3},{8,10},{9,13},{10,... | collective-permute-start | bytes 147464 | tf_op jit(solution)/shard_map/ppermute | solution.py:225
  29.5 5.6 %collective-permute-start.4 = (s16[6,16,128]{2,1,0:T(8,128)(2,1)S(1)}, s16[6,16,128]{2,1,0:T(8,128)(2,1)S(1)}, u32[]{:S(2)}, u32[]{:S(2)}) collective-permute-start(s16[6,16,128]{2,1,0:T(8,128)(2,1)S(1)} %minimum_convert_fusion.11), channel_id=1, source_target_pairs={{0,16},{1,17},{2,18},{3,19},{4,20},{5,21},{6,22},{7,23},{8,24},{9,... | collective-permute-start | bytes 73736 | tf_op jit(solution)/shard_map/ppermute | solution.py:225
  31.2 4.8 %collective-permute-start.8 = (s16[6,16,128]{2,1,0:T(8,128)(2,1)S(1)}, s16[6,16,128]{2,1,0:T(8,128)(2,1)S(1)}, u32[]{:S(2)}, u32[]{:S(2)}) collective-permute-start(s16[6,16,128]{2,1,0:T(8,128)(2,1)S(1)} %minimum_convert_fusion.10), channel_id=1, source_target_pairs={{0,16},{1,17},{2,18},{3,19},{4,20},{5,21},{6,22},{7,23},{8,24},{9,... | collective-permute-start | bytes 73736 | tf_op jit(solution)/shard_map/ppermute | solution.py:225
  32.6 2.4 %copy-start.7 = (s32[6,2]{0,1:T(2,128)S(1)}, s32[6,2]{0,1:T(2,128)}, u32[]{:S(2)}) copy-start(s32[6,2]{0,1:T(2,128)} %param.25) | copy-start | bytes 148
  32.6 4.8 %collective-permute-start.12 = (s16[6,16,128]{2,1,0:T(8,128)(2,1)S(1)}, s16[6,16,128]{2,1,0:T(8,128)(2,1)S(1)}, u32[]{:S(2)}, u32[]{:S(2)}) collective-permute-start(s16[6,16,128]{2,1,0:T(8,128)(2,1)S(1)} %minimum_convert_fusion.9), channel_id=1, source_target_pairs={{0,16},{1,17},{2,18},{3,19},{4,20},{5,21},{6,22},{7,23},{8,24},{9,... | collective-permute-start | bytes 73736 | tf_op jit(solution)/shard_map/ppermute | solution.py:225
  34.4 3.9 %copy-start.5 = (f32[768]{0:T(1024)S(1)}, f32[768]{0:T(1024)}, u32[]{:S(2)}) copy-start(f32[768]{0:T(1024)} %param.22) | copy-start | bytes 9220
  34.4 3.9 %copy-start.6 = (f32[768]{0:T(1024)S(1)}, f32[768]{0:T(1024)}, u32[]{:S(2)}) copy-start(f32[768]{0:T(1024)} %param.23) | copy-start | bytes 9220
  34.4 3.9 %collective-permute-start.16 = (s16[6,16,128]{2,1,0:T(8,128)(2,1)S(1)}, s16[6,16,128]{2,1,0:T(8,128)(2,1)S(1)}, u32[]{:S(2)}, u32[]{:S(2)}) collective-permute-start(s16[6,16,128]{2,1,0:T(8,128)(2,1)S(1)} %minimum_convert_fusion.8), channel_id=1, source_target_pairs={{0,4},{1,3},{2,6},{3,1},{4,0},{5,7},{6,2},{7,5},{8,12},{9,11},{10,... | collective-permute-start | bytes 73736 | tf_op jit(solution)/shard_map/ppermute | solution.py:225

commit v5 on v4

--- a/solution.py
+++ b/solution.py
@@ -13,7 +13,7 @@
 TOP = 40.0
 SCALE = 65535.0 / TOP
 HALF = 32768
-VMEM_SUMS = 56
+VMEM_SUMS = 24
 
 
 def encode(sums):
@@ -40,8 +40,8 @@
 def block_sums_kernel(parts, owned, chunks, *refs):
     count = len(parts)
     in_refs, refs = refs[:9], refs[9:]
-    send_refs, keep_refs, sum_refs, coded_refs = (refs[i * count : (i + 1) * count] for i in range(4))
-    *held, small_sems, sems, out_sems = refs[4 * count :]
+    send_refs, keep_refs, sum_refs = (refs[i * count : (i + 1) * count] for i in range(3))
+    *held, small_sems, sems = refs[3 * count :]
     owner_ref, sub_ref, factor_ref, scale_ref, sigma_ref, weight_ref, slot_ref, idio_ref, loads_ref = held
     half = keep_refs[0].shape[0]
     tiles = scale_ref.shape[0]
@@ -91,28 +91,17 @@
                     code = jnp.where(core == 0, relative_code(rel, order[0]), relative_code(rel, order[1]))
                     sum_ref[code * owned + sub_ref[k]] += sums[first : first + years]
 
-    out = []
-    piece = half // PIECES
-    for i in range(PIECES):
-        at = pl.ds(i * piece, piece)
-        for p, (send_ref, keep_ref, sum_ref, coded_ref) in enumerate(zip(send_refs, keep_refs, sum_refs, coded_refs)):
-
-            def body(b, carry):
-                coded_ref[b] = encode(sum_ref[b])
-                coded_ref[half + b] = encode(sum_ref[half + b])
-                return carry
-
-            lax.fori_loop(i * piece, (i + 1) * piece, body, 0, unroll=2)
-            for j, (source, target) in enumerate(((coded_ref.at[pl.ds(half + i * piece, piece)], send_ref), (coded_ref.at[at], keep_ref))):
-                copy = pltpu.make_async_copy(source, target.at[at], out_sems.at[p, i, j])
-                copy.start()
-                out.append(copy)
-    for copy in out:
-        copy.wait()
+    for send_ref, keep_ref, sum_ref in zip(send_refs, keep_refs, sum_refs):
+
+        def body(b, carry):
+            send_ref[b] = encode(sum_ref[half + b])
+            keep_ref[b] = encode(sum_ref[b])
+            return carry
+
+        lax.fori_loop(0, half, body, 0, unroll=4)
 
 
 GROUP = 16
-PIECES = 2
 
 
 def block_sums(parts, idio, factor, loads, log_scale, sigma, weight, slot, owner, sub, blocks, owned, chunks=2):
@@ -124,19 +113,17 @@
     out = pl.pallas_call(
         functools.partial(block_sums_kernel, parts, owned, chunks),
         in_specs=[hbm] * len(inputs),
-        out_specs=[hbm] * (2 * len(parts)),
+        out_specs=[pl.BlockSpec(memory_space=pltpu.VMEM)] * (2 * len(parts)),
         out_shape=[jax.ShapeDtypeStruct(s, jnp.int16) for s in shapes * 2],
         scratch_shapes=[pltpu.VMEM((blocks, years, TB), jnp.float32) for _, years, _ in parts]
-        + [pltpu.VMEM((blocks, years, TB), jnp.int16) for _, years, _ in parts]
         + [pltpu.SMEM(a.shape, a.dtype) for a in inputs[:2]]
         + [pltpu.VMEM(a.shape, a.dtype) for a in inputs[2:]]
         + [
             pltpu.SemaphoreType.DMA((7,)),
             pltpu.SemaphoreType.DMA((2, chunks)),
-            pltpu.SemaphoreType.DMA((len(parts), PIECES, 2)),
         ],
         compiler_params=pltpu.CompilerParams(vmem_limit_bytes=VMEM_SUMS * 2**20),
-    )(*inputs)
+    )(*(pltpu.with_memory_space_constraint(a, pltpu.HBM) for a in inputs))
     return out[: len(parts)], out[len(parts) :]
 
 
@@ -199,7 +186,7 @@
     return jnp.concatenate([jnp.sum(pieces[:, :, h * years : (h + 1) * years], axis=0) for h in range(2)], axis=0).T
 
 
-PARTS = ((0, 16, ((0, 1, 2, 3), (1, 0, 2, 3))), (16, 16, ((0, 1, 2, 3), (1, 0, 2, 3))), (32, 16, ((0, 1, 2, 3), (1, 0, 2, 3))), (48, 16, ((2, 3, 0, 1), (2, 3, 1, 0))),)
+PARTS = ((0, 32, ((0, 1, 2, 3), (1, 0, 2, 3))), (32, 16, ((0, 1, 2, 3), (1, 0, 2, 3))), (48, 16, ((2, 3, 0, 1), (2, 3, 1, 0))),)
 
 
 def dense_on_device(

time: 52.9 us -> 51.2 us (0.968)
  waiting for transfers between devices: 4.54 us -> 10.3 us
  starting transfers between devices: 25.7 us -> 20.4 us
  Pallas kernels: 7.19 us -> 6.18 us
  other arithmetic: 2.27 us -> 1.35 us
    ppermute x16 -> x12, waiting for transfers between devices: 4.53 us -> 10.3 us  [dense_on_device(): received[p].append(lax.ppermute(sends[p], ('risk', 'tcol'), pairs))]
    ppermute x16 -> x12, starting transfers between devices: 25.7 us -> 20.4 us  [dense_on_device(): received[p].append(lax.ppermute(sends[p], ('risk', 'tcol'), pairs))]
    pallas_call x1, Pallas kernels: 5.62 us -> 4.58 us  [block_sums(): pl.pallas_call(functools.partial(block_sums_kernel, parts, owned, chunks)...]
    convert_element_type x12 -> x9, other arithmetic: 1.56 us -> 0.65 us  [add_coded(): return jnp.minimum(steps, HALF - 1).astype(jnp.int16)]
  transfers between devices with their start and end apart: 17 -> 13, of which waited for: 5 -> 6; matrix products, arithmetic and copies ran while one was open for 3% -> 1% of each run, Pallas kernels for 0% -> 0%
where the time goes in v5:
time: 51.2 us; the launch traced here: 51 us
  starting transfers between devices  20.4 us (40%)
  blocking collectives  11.9 us (23%)
  waiting for transfers between devices  10.3 us (20%)
  Pallas kernels  6.18 us (12%)
  other arithmetic  1.35 us (3%)
  between operations  0.73 us (1%)
    ppermute x12, starting transfers between devices, dense_on_device(): received[p].append(lax.ppermute(sends[p], ('risk', 'tcol'), pairs))  20.4 us
    all_to_all x1, blocking collectives, dense_on_device(): lax.all_to_all(pieces, 'risk', split_axis=0, concat_axis=0, tiled=True)  11.9 us
    ppermute x12, waiting for transfers between devices, dense_on_device(): received[p].append(lax.ppermute(sends[p], ('risk', 'tcol'), pairs))  10.3 us
    pallas_call x1, Pallas kernels, block_sums(): pl.pallas_call(functools.partial(block_sums_kernel, parts, owned, chunks)...  4.58 us
    pallas_call x1, Pallas kernels, retro(): pl.pallas_call(functools.partial(retro_kernel, parts), grid=(1,), in_spec...  1.59 us
  transfers between devices with their start and end apart: 13, of which 6 were waited for; matrix products, arithmetic and copies ran while one was open for 1% of the time, Pallas kernels for 0%

profile of v5, /device:TPU:0, one launch (start us, length us, event | category | flops | bytes accessed | tf_op | source)
XLA Modules:
  0.0 51.0 jit_solution(18184411135279896214)
XLA Ops:
  0.6 0.0 copy-start
  0.6 4.6 %shard_map.140 = (s16[48,32,128]{2,1,0:T(8,128)(2,1)S(1)}, s16[48,16,128]{2,1,0:T(8,128)(2,1)S(1)}, s16[48,16,128]{2,1,0:T(8,128)(2,1)S(1)}, s16[48,32,128]{2,1,...) custom-call(s32[64]{0:T(128)} %bitcast.15, s32[64]{0:T(128)} %refs_1_.1, ...), custom_call_target="tpu_custom_call" | custom-call | tf_op jit(solution)/shard_map/pallas_call | solution.py:113
  5.2 3.0 %collective-permute-start.5 = (s16[48,16,128]{2,1,0:T(8,128)(2,1)S(1)}, s16[48,16,128]{2,1,0:T(8,128)(2,1)S(1)}, u32[]{:S(2)}, u32[]{:S(2)}) collective-permute-start(s16[48,16,128]{2,1,0:T(8,128)(2,1)S(1)} %get-tuple-element.13), channel_id=1, source_target_pairs={{0,2},{1,5},{2,0},{3,7},{4,6},{5,1},{6,4},{7,3},{8,10},{9,13},{10,... | collective-permute-start | bytes 589832 | tf_op jit(solution)/shard_map/ppermute | solution.py:212
  8.3 0.0 copy-done
  8.3 0.0 collective-permute-start
  8.3 1.6 %collective-permute-start.9 = (s16[48,16,128]{2,1,0:T(8,128)(2,1)S(1)}, s16[48,16,128]{2,1,0:T(8,128)(2,1)S(1)}, u32[]{:S(2)}, u32[]{:S(2)}) collective-permute-start(s16[48,16,128]{2,1,0:T(8,128)(2,1)S(1)} %get-tuple-element.15), channel_id=1, source_target_pairs={{0,8},{1,9},{2,10},{3,11},{4,12},{5,13},{6,14},{7,15},{8,0},{9,1},... | collective-permute-start | bytes 589832 | tf_op jit(solution)/shard_map/ppermute | solution.py:212
  9.8 1.1 %collective-permute-start.1 = (s16[48,32,128]{2,1,0:T(8,128)(2,1)S(1)}, s16[48,32,128]{2,1,0:T(8,128)(2,1)S(1)}, u32[]{:S(2)}, u32[]{:S(2)}) collective-permute-start(s16[48,32,128]{2,1,0:T(8,128)(2,1)S(1)} %get-tuple-element.11), channel_id=1, source_target_pairs={{0,2},{1,5},{2,0},{3,7},{4,6},{5,1},{6,4},{7,3},{8,10},{9,13},{10,... | collective-permute-start | bytes 1179656 | tf_op jit(solution)/shard_map/ppermute | solution.py:212
  10.9 1.0 %collective-permute-done.5.refs_6_ = s16[48,16,128]{2,1,0:T(8,128)(2,1)S(1)} collective-permute-done((s16[48,16,128]{2,1,0:T(8,128)(2,1)S(1)}, s16[48,16,128]{2,1,0:T(8,128)(2,1)S(1)}, u32[]{:S(2)}, u32[]{:S(2)}) %collective-permute-start.5) | collective-permute-done | bytes 196640 | tf_op jit(solution)/shard_map/ppermute | solution.py:212
  11.9 0.1 minimum_convert_fusion.2
  12.0 2.1 %collective-permute-start.6 = (s16[24,16,128]{2,1,0:T(8,128)(2,1)S(1)}, s16[24,16,128]{2,1,0:T(8,128)(2,1)S(1)}, u32[]{:S(2)}, u32[]{:S(2)}) collective-permute-start(s16[24,16,128]{2,1,0:T(8,128)(2,1)S(1)} %minimum_convert_fusion.2), channel_id=1, source_target_pairs={{0,4},{1,3},{2,6},{3,1},{4,0},{5,7},{6,2},{7,5},{8,12},{9,11},{10,... | collective-permute-start | bytes 294920 | tf_op jit(solution)/shard_map/ppermute | solution.py:212
  14.1 1.5 %collective-permute-done.9.refs_11_ = s16[48,16,128]{2,1,0:T(8,128)(2,1)S(1)} collective-permute-done((s16[48,16,128]{2,1,0:T(8,128)(2,1)S(1)}, s16[48,16,128]{2,1,0:T(8,128)(2,1)S(1)}, u32[]{:S(2)}, u32[]{:S(2)}) %collective-permute-start.9) | collective-permute-done | bytes 196640 | tf_op jit(solution)/shard_map/ppermute | solution.py:212
  15.6 0.1 minimum_convert_fusion.1
  15.7 2.6 %collective-permute-start.10 = (s16[24,16,128]{2,1,0:T(8,128)(2,1)S(1)}, s16[24,16,128]{2,1,0:T(8,128)(2,1)S(1)}, u32[]{:S(2)}, u32[]{:S(2)}) collective-permute-start(s16[24,16,128]{2,1,0:T(8,128)(2,1)S(1)} %minimum_convert_fusion.1), channel_id=1, source_target_pairs={{0,16},{1,17},{2,18},{3,19},{4,20},{5,21},{6,22},{7,23},{8,24},{9,... | collective-permute-start | bytes 294920 | tf_op jit(solution)/shard_map/ppermute | solution.py:212
  18.3 0.0 collective-permute-done.6.refs_7_
  18.3 0.1 minimum_convert_fusion.5
  18.4 1.7 %collective-permute-start.7 = (s16[12,16,128]{2,1,0:T(8,128)(2,1)S(1)}, s16[12,16,128]{2,1,0:T(8,128)(2,1)S(1)}, u32[]{:S(2)}, u32[]{:S(2)}) collective-permute-start(s16[12,16,128]{2,1,0:T(8,128)(2,1)S(1)} %minimum_convert_fusion.5), channel_id=1, source_target_pairs={{0,8},{1,9},{2,10},{3,11},{4,12},{5,13},{6,14},{7,15},{8,0},{9,1},... | collective-permute-start | bytes 147464 | tf_op jit(solution)/shard_map/ppermute | solution.py:212
  20.0 0.0 collective-permute-done.1.refs_1_
  20.0 0.1 minimum_convert_fusion
  20.2 1.6 %collective-permute-start.2 = (s16[24,32,128]{2,1,0:T(8,128)(2,1)S(1)}, s16[24,32,128]{2,1,0:T(8,128)(2,1)S(1)}, u32[]{:S(2)}, u32[]{:S(2)}) collective-permute-start(s16[24,32,128]{2,1,0:T(8,128)(2,1)S(1)} %minimum_convert_fusion), channel_id=1, source_target_pairs={{0,4},{1,3},{2,6},{3,1},{4,0},{5,7},{6,2},{7,5},{8,12},{9,11},{10,... | collective-permute-start | bytes 589832 | tf_op jit(solution)/shard_map/ppermute | solution.py:212
  21.7 1.4 %collective-permute-done.10.refs_12_ = s16[24,16,128]{2,1,0:T(8,128)(2,1)S(1)} collective-permute-done((s16[24,16,128]{2,1,0:T(8,128)(2,1)S(1)}, s16[24,16,128]{2,1,0:T(8,128)(2,1)S(1)}, u32[]{:S(2)}, u32[]{:S(2)}) %collective-permute-start.10) | collective-permute-done | bytes 98336 | tf_op jit(solution)/shard_map/ppermute | solution.py:212
  23.1 0.1 minimum_convert_fusion.4
  23.2 0.2 collective-permute-start.11
  23.4 2.5 %collective-permute-done.2.refs_2_ = s16[24,32,128]{2,1,0:T(8,128)(2,1)S(1)} collective-permute-done((s16[24,32,128]{2,1,0:T(8,128)(2,1)S(1)}, s16[24,32,128]{2,1,0:T(8,128)(2,1)S(1)}, u32[]{:S(2)}, u32[]{:S(2)}) %collective-permute-start.2) | collective-permute-done | bytes 196640 | tf_op jit(solution)/shard_map/ppermute | solution.py:212
  25.9 0.1 minimum_convert_fusion.3
  26.0 0.5 collective-permute-start.3
  26.5 0.0 collective-permute-done.7.refs_8_
  26.5 2.3 %collective-permute-start.8 = (s16[6,16,128]{2,1,0:T(8,128)(2,1)S(1)}, s16[6,16,128]{2,1,0:T(8,128)(2,1)S(1)}, u32[]{:S(2)}, u32[]{:S(2)}) collective-permute-start(s16[6,16,128]{2,1,0:T(8,128)(2,1)S(1)} %minimum_convert_fusion.8), channel_id=1, source_target_pairs={{0,16},{1,17},{2,18},{3,19},{4,20},{5,21},{6,22},{7,23},{8,24},{9,... | collective-permute-start | bytes 73736 | tf_op jit(solution)/shard_map/ppermute | solution.py:212
  28.8 1.9 %collective-permute-done.3.refs_3_ = s16[12,32,128]{2,1,0:T(8,128)(2,1)S(1)} collective-permute-done((s16[12,32,128]{2,1,0:T(8,128)(2,1)S(1)}, s16[12,32,128]{2,1,0:T(8,128)(2,1)S(1)}, u32[]{:S(2)}, u32[]{:S(2)}) %collective-permute-start.3) | collective-permute-done | bytes 98336 | tf_op jit(solution)/shard_map/ppermute | solution.py:212
  30.7 0.1 minimum_convert_fusion.6
  30.7 0.0 copy-start.3
  30.8 2.0 %collective-permute-start.4 = (s16[6,32,128]{2,1,0:T(8,128)(2,1)S(1)}, s16[6,32,128]{2,1,0:T(8,128)(2,1)S(1)}, u32[]{:S(2)}, u32[]{:S(2)}) collective-permute-start(s16[6,32,128]{2,1,0:T(8,128)(2,1)S(1)} %minimum_convert_fusion.6), channel_id=1, source_target_pairs={{0,16},{1,17},{2,18},{3,19},{4,20},{5,21},{6,22},{7,23},{8,24},{9,... | collective-permute-start | bytes 147464 | tf_op jit(solution)/shard_map/ppermute | solution.py:212
  32.8 0.0 collective-permute-done.11.refs_13_
  32.8 0.0 copy-start.1
  32.8 0.0 copy-start.2
  32.8 1.8 %collective-permute-start.12 = (s16[6,16,128]{2,1,0:T(8,128)(2,1)S(1)}, s16[6,16,128]{2,1,0:T(8,128)(2,1)S(1)}, u32[]{:S(2)}, u32[]{:S(2)}) collective-permute-start(s16[6,16,128]{2,1,0:T(8,128)(2,1)S(1)} %minimum_convert_fusion.7), channel_id=1, source_target_pairs={{0,4},{1,3},{2,6},{3,1},{4,0},{5,7},{6,2},{7,5},{8,12},{9,11},{10,... | collective-permute-start | bytes 73736 | tf_op jit(solution)/shard_map/ppermute | solution.py:212
  34.7 0.0 copy-done.3
  34.7 0.1 copy.15.rblock_ref
  34.8 0.0 collective-permute-done.other_ref
  34.8 0.0 collective-permute-done.8.refs_9_
  34.8 1.9 %collective-permute-done.12.refs_14_ = s16[6,16,128]{2,1,0:T(8,128)(2,1)S(1)} collective-permute-done((s16[6,16,128]{2,1,0:T(8,128)(2,1)S(1)}, s16[6,16,128]{2,1,0:T(8,128)(2,1)S(1)}, u32[]{:S(2)}, u32[]{:S(2)}) %collective-permute-start.12) | collective-permute-done | bytes 24608 | tf_op jit(solution)/shard_map/ppermute | solution.py:212
  36.7 0.0 collective-permute-done.4.refs_4_
  36.7 0.0 copy-done.1
  36.7 0.0 copy-done.2
  36.7 1.6 %shard_map.141 = (f32[64,768]{1,0:T(8,128)}, f32[16,16,128]{2,1,0:T(8,128)S(1)}) custom-call(s32[6,2]{1,0:T(8,128)S(1)} %copy.15.rblock_ref, f32[6,128]{1,0:T(8,128)S(1)} %bitcast.9, f32[6,128]{1,0:T(8,128)S(1)} %bitcast.10, bf16[6,2,64,128]{3,2,1,0:T(8,128)(2,1)S(1)} %copy-done, bf16[6,2,64,128]{3,2,1,0:T(8,128)(2,1)S(1)} %collective-permute-done.other_ref, ...), custom_call_target="tpu_custom_call" | custom-call | tf_op jit(solution)/shard_map/pallas_call | solution.py:171
  38.3 11.9 %all_to_all.5 = f32[16,16,128]{2,1,0:T(8,128)S(1)} all-to-all(f32[16,16,128]{2,1,0:T(8,128)S(1)} %get-tuple-element.17), channel_id=1, replica_groups=mesh['risk'=16,'tcol'=2] {'risk'}, dimensions={0} | all-to-all | bytes 262144 | tf_op jit(solution)/shard_map/all_to_all | solution.py:219
  50.2 0.1 slice_reduce_fusion.1
  50.3 0.6 %maximum_bitcast_fusion = f32[64,32]{0,1:T(8,128)} fusion(f32[16,64]{1,0:T(8,128)S(1)} %get-tuple-element.19, f32[16,64]{1,0:T(8,128)S(1)} %get-tuple-element.18), kind=kLoop, calls=%fused_computation.11 | loop fusion | flops 2048 | bytes 16384 | tf_op jit(solution)/shard_map/transpose | solution.py:186
  (2 shorter events, 0.1 us)
Async XLA Ops:
  0.6 7.6 %copy-start = (bf16[6,2,64,128]{3,2,1,0:T(8,128)(2,1)S(1)}, bf16[6,2,64,128]{3,2,1,0:T(8,128)(2,1)}, u32[]{:S(2)}) copy-start(bf16[6,2,64,128]{3,2,1,0:T(8,128)(2,1)} %mine_ref.1) | copy-start | bytes 589828
  5.2 6.7 %collective-permute-start.5 = (s16[48,16,128]{2,1,0:T(8,128)(2,1)S(1)}, s16[48,16,128]{2,1,0:T(8,128)(2,1)S(1)}, u32[]{:S(2)}, u32[]{:S(2)}) collective-permute-start(s16[48,16,128]{2,1,0:T(8,128)(2,1)S(1)} %get-tuple-element.13), channel_id=1, source_target_pairs={{0,2},{1,5},{2,0},{3,7},{4,6},{5,1},{6,4},{7,3},{8,10},{9,13},{10,... | collective-permute-start | bytes 589832 | tf_op jit(solution)/shard_map/ppermute | solution.py:212
  8.3 26.5 %collective-permute-start = (bf16[6,2,64,128]{3,2,1,0:T(8,128)(2,1)S(1)}, bf16[6,2,64,128]{3,2,1,0:T(8,128)(2,1)S(1)}, u32[]{:S(2)}, u32[]{:S(2)}) collective-permute-start(bf16[6,2,64,128]{3,2,1,0:T(8,128)(2,1)S(1)} %copy-done), channel_id=1, source_target_pairs={{0,1},{1,0},{2,3},{3,2},{4,5},{5,4},{6,7},{7,6},{8,9},{9,8},{10,11... | collective-permute-start | bytes 589832 | tf_op jit(solution)/shard_map/ppermute | solution.py:198
  8.3 7.3 %collective-permute-start.9 = (s16[48,16,128]{2,1,0:T(8,128)(2,1)S(1)}, s16[48,16,128]{2,1,0:T(8,128)(2,1)S(1)}, u32[]{:S(2)}, u32[]{:S(2)}) collective-permute-start(s16[48,16,128]{2,1,0:T(8,128)(2,1)S(1)} %get-tuple-element.15), channel_id=1, source_target_pairs={{0,8},{1,9},{2,10},{3,11},{4,12},{5,13},{6,14},{7,15},{8,0},{9,1},... | collective-permute-start | bytes 589832 | tf_op jit(solution)/shard_map/ppermute | solution.py:212
  9.8 10.2 %collective-permute-start.1 = (s16[48,32,128]{2,1,0:T(8,128)(2,1)S(1)}, s16[48,32,128]{2,1,0:T(8,128)(2,1)S(1)}, u32[]{:S(2)}, u32[]{:S(2)}) collective-permute-start(s16[48,32,128]{2,1,0:T(8,128)(2,1)S(1)} %get-tuple-element.11), channel_id=1, source_target_pairs={{0,2},{1,5},{2,0},{3,7},{4,6},{5,1},{6,4},{7,3},{8,10},{9,13},{10,... | collective-permute-start | bytes 1179656 | tf_op jit(solution)/shard_map/ppermute | solution.py:212
  12.0 6.3 %collective-permute-start.6 = (s16[24,16,128]{2,1,0:T(8,128)(2,1)S(1)}, s16[24,16,128]{2,1,0:T(8,128)(2,1)S(1)}, u32[]{:S(2)}, u32[]{:S(2)}) collective-permute-start(s16[24,16,128]{2,1,0:T(8,128)(2,1)S(1)} %minimum_convert_fusion.2), channel_id=1, source_target_pairs={{0,4},{1,3},{2,6},{3,1},{4,0},{5,7},{6,2},{7,5},{8,12},{9,11},{10,... | collective-permute-start | bytes 294920 | tf_op jit(solution)/shard_map/ppermute | solution.py:212
  15.7 7.5 %collective-permute-start.10 = (s16[24,16,128]{2,1,0:T(8,128)(2,1)S(1)}, s16[24,16,128]{2,1,0:T(8,128)(2,1)S(1)}, u32[]{:S(2)}, u32[]{:S(2)}) collective-permute-start(s16[24,16,128]{2,1,0:T(8,128)(2,1)S(1)} %minimum_convert_fusion.1), channel_id=1, source_target_pairs={{0,16},{1,17},{2,18},{3,19},{4,20},{5,21},{6,22},{7,23},{8,24},{9,... | collective-permute-start | bytes 294920 | tf_op jit(solution)/shard_map/ppermute | solution.py:212
  18.4 8.2 %collective-permute-start.7 = (s16[12,16,128]{2,1,0:T(8,128)(2,1)S(1)}, s16[12,16,128]{2,1,0:T(8,128)(2,1)S(1)}, u32[]{:S(2)}, u32[]{:S(2)}) collective-permute-start(s16[12,16,128]{2,1,0:T(8,128)(2,1)S(1)} %minimum_convert_fusion.5), channel_id=1, source_target_pairs={{0,8},{1,9},{2,10},{3,11},{4,12},{5,13},{6,14},{7,15},{8,0},{9,1},... | collective-permute-start | bytes 147464 | tf_op jit(solution)/shard_map/ppermute | solution.py:212
  20.2 5.7 %collective-permute-start.2 = (s16[24,32,128]{2,1,0:T(8,128)(2,1)S(1)}, s16[24,32,128]{2,1,0:T(8,128)(2,1)S(1)}, u32[]{:S(2)}, u32[]{:S(2)}) collective-permute-start(s16[24,32,128]{2,1,0:T(8,128)(2,1)S(1)} %minimum_convert_fusion), channel_id=1, source_target_pairs={{0,4},{1,3},{2,6},{3,1},{4,0},{5,7},{6,2},{7,5},{8,12},{9,11},{10,... | collective-permute-start | bytes 589832 | tf_op jit(solution)/shard_map/ppermute | solution.py:212
  23.2 9.6 %collective-permute-start.11 = (s16[12,16,128]{2,1,0:T(8,128)(2,1)S(1)}, s16[12,16,128]{2,1,0:T(8,128)(2,1)S(1)}, u32[]{:S(2)}, u32[]{:S(2)}) collective-permute-start(s16[12,16,128]{2,1,0:T(8,128)(2,1)S(1)} %minimum_convert_fusion.4), channel_id=1, source_target_pairs={{0,2},{1,5},{2,0},{3,7},{4,6},{5,1},{6,4},{7,3},{8,10},{9,13},{10,... | collective-permute-start | bytes 147464 | tf_op jit(solution)/shard_map/ppermute | solution.py:212
  26.0 4.7 %collective-permute-start.3 = (s16[12,32,128]{2,1,0:T(8,128)(2,1)S(1)}, s16[12,32,128]{2,1,0:T(8,128)(2,1)S(1)}, u32[]{:S(2)}, u32[]{:S(2)}) collective-permute-start(s16[12,32,128]{2,1,0:T(8,128)(2,1)S(1)} %minimum_convert_fusion.3), channel_id=1, source_target_pairs={{0,8},{1,9},{2,10},{3,11},{4,12},{5,13},{6,14},{7,15},{8,0},{9,1},... | collective-permute-start | bytes 294920 | tf_op jit(solution)/shard_map/ppermute | solution.py:212
  26.5 8.2 %collective-permute-start.8 = (s16[6,16,128]{2,1,0:T(8,128)(2,1)S(1)}, s16[6,16,128]{2,1,0:T(8,128)(2,1)S(1)}, u32[]{:S(2)}, u32[]{:S(2)}) collective-permute-start(s16[6,16,128]{2,1,0:T(8,128)(2,1)S(1)} %minimum_convert_fusion.8), channel_id=1, source_target_pairs={{0,16},{1,17},{2,18},{3,19},{4,20},{5,21},{6,22},{7,23},{8,24},{9,... | collective-permute-start | bytes 73736 | tf_op jit(solution)/shard_map/ppermute | solution.py:212
  30.7 3.9 %copy-start.3 = (s32[6,2]{0,1:T(2,128)S(1)}, s32[6,2]{0,1:T(2,128)}, u32[]{:S(2)}) copy-start(s32[6,2]{0,1:T(2,128)} %param.25) | copy-start | bytes 148
  30.8 6.0 %collective-permute-start.4 = (s16[6,32,128]{2,1,0:T(8,128)(2,1)S(1)}, s16[6,32,128]{2,1,0:T(8,128)(2,1)S(1)}, u32[]{:S(2)}, u32[]{:S(2)}) collective-permute-start(s16[6,32,128]{2,1,0:T(8,128)(2,1)S(1)} %minimum_convert_fusion.6), channel_id=1, source_target_pairs={{0,16},{1,17},{2,18},{3,19},{4,20},{5,21},{6,22},{7,23},{8,24},{9,... | collective-permute-start | bytes 147464 | tf_op jit(solution)/shard_map/ppermute | solution.py:212
  32.8 3.9 %copy-start.1 = (f32[768]{0:T(1024)S(1)}, f32[768]{0:T(1024)}, u32[]{:S(2)}) copy-start(f32[768]{0:T(1024)} %param.22) | copy-start | bytes 9220
  32.8 3.9 %copy-start.2 = (f32[768]{0:T(1024)S(1)}, f32[768]{0:T(1024)}, u32[]{:S(2)}) copy-start(f32[768]{0:T(1024)} %param.23) | copy-start | bytes 9220
  32.8 3.9 %collective-permute-start.12 = (s16[6,16,128]{2,1,0:T(8,128)(2,1)S(1)}, s16[6,16,128]{2,1,0:T(8,128)(2,1)S(1)}, u32[]{:S(2)}, u32[]{:S(2)}) collective-permute-start(s16[6,16,128]{2,1,0:T(8,128)(2,1)S(1)} %minimum_convert_fusion.7), channel_id=1, source_target_pairs={{0,4},{1,3},{2,6},{3,1},{4,0},{5,7},{6,2},{7,5},{8,12},{9,11},{10,... | collective-permute-start | bytes 73736 | tf_op jit(solution)/shard_map/ppermute | solution.py:212

commit v6 on v5

--- a/solution.py
+++ b/solution.py
@@ -145,16 +145,14 @@
             mine, other = mine_ref[g, k], other_ref[g, k]
             top = jnp.where(first, mine, other)
             bottom = jnp.where(first, other, mine)
-            part = lax.dot_general(
-                jnp.concatenate([top, bottom], axis=0), low, (((0,), (1,)), ((), ())),
-                preferred_element_type=jnp.float32,
-            )
+            part = jnp.dot(low, jnp.concatenate([top, bottom], axis=0), preferred_element_type=jnp.float32)
             acc_ref[rblock_ref[g, k]] += part
     wide = RB // 4
     for q in range(acc_ref.shape[0]):
+        turned = acc_ref[q].T
         for i in range(4):
             for h in range(2):
-                out_ref[4 * q + i, :, h * 64 : (h + 1) * 64] = acc_ref[q, pl.ds(i * wide + h * wide // 2, wide // 2), :]
+                out_ref[4 * q + i, :, h * 64 : (h + 1) * 64] = turned[i * wide + h * wide // 2 : i * wide + (h + 1) * wide // 2]
 
 
 def retro(parts, inbound, attach, limit, mine, other, rblock):
@@ -176,7 +174,7 @@
         + [first(a) for a in inbound],
         out_specs=[whole(a) for a in outs],
         out_shape=outs,
-        scratch_shapes=[pltpu.VMEM((REINS // RB, RB, years), jnp.float32)],
+        scratch_shapes=[pltpu.VMEM((REINS // RB, years, RB), jnp.float32)],
         compiler_params=pltpu.CompilerParams(vmem_limit_bytes=20 * 2**20),
     )(rblock, attach, limit, mine, other, *inbound)
 
@@ -186,7 +184,12 @@
     return jnp.concatenate([jnp.sum(pieces[:, :, h * years : (h + 1) * years], axis=0) for h in range(2)], axis=0).T
 
 
-PARTS = ((0, 32, ((0, 1, 2, 3), (1, 0, 2, 3))), (32, 16, ((0, 1, 2, 3), (1, 0, 2, 3))), (48, 16, ((2, 3, 0, 1), (2, 3, 1, 0))),)
+PARTS = (
+    (0, 16, ((2, 3, 0, 1), (2, 3, 1, 0))),
+    (16, 16, ((0, 1, 2, 3), (1, 0, 2, 3))),
+    (32, 16, ((1, 0, 2, 3), (0, 1, 2, 3))),
+    (48, 16, ((1, 0, 2, 3), (0, 1, 2, 3))),
+)
 
 
 def dense_on_device(

time: 51.2 us -> 49.9 us (0.975)
  waiting for transfers between devices: 10.3 us -> 3.95 us
  starting transfers between devices: 20.4 us -> 25.5 us
    ppermute x12 -> x16, waiting for transfers between devices: 10.3 us -> 3.95 us  [dense_on_device(): received[p].append(lax.ppermute(sends[p], ('risk', 'tcol'), pairs))]
    ppermute x12 -> x16, starting transfers between devices: 20.4 us -> 25.5 us  [dense_on_device(): received[p].append(lax.ppermute(sends[p], ('risk', 'tcol'), pairs))]
  transfers between devices with their start and end apart: 13 -> 17, of which waited for: 6 -> 4; matrix products, arithmetic and copies ran while one was open for 1% -> 2% of each run, Pallas kernels for 0% -> 0%
where the time goes in v6:
time: 49.9 us; the launch traced here: 49.8 us
  starting transfers between devices  25.5 us (51%)
  blocking collectives  11.9 us (24%)
  Pallas kernels  6.13 us (12%)
  waiting for transfers between devices  3.95 us (8%)
  other arithmetic  1.37 us (3%)
  between operations  0.74 us (1%)
    ppermute x16, starting transfers between devices, dense_on_device(): received[p].append(lax.ppermute(sends[p], ('risk', 'tcol'), pairs))  25.5 us
    all_to_all x1, blocking collectives, dense_on_device(): lax.all_to_all(pieces, 'risk', split_axis=0, concat_axis=0, tiled=True)  11.9 us
    pallas_call x1, Pallas kernels, block_sums(): pl.pallas_call(functools.partial(block_sums_kernel, parts, owned, chunks)...  4.63 us
    ppermute x16, waiting for transfers between devices, dense_on_device(): received[p].append(lax.ppermute(sends[p], ('risk', 'tcol'), pairs))  3.95 us
    pallas_call x1, Pallas kernels, retro(): pl.pallas_call(functools.partial(retro_kernel, parts), grid=(1,), in_spec...  1.5 us
  transfers between devices with their start and end apart: 17, of which 4 were waited for; matrix products, arithmetic and copies ran while one was open for 2% of the time, Pallas kernels for 0%

profile of v6, /device:TPU:0, one launch (start us, length us, event | category | flops | bytes accessed | tf_op | source)
XLA Modules:
  0.0 49.8 jit_solution(14116666514736870832)
XLA Ops:
  0.6 0.0 copy-start
  0.6 4.6 %shard_map.140 = (s16[48,16,128]{2,1,0:T(8,128)(2,1)S(1)}, s16[48,16,128]{2,1,0:T(8,128)(2,1)S(1)}, s16[48,16,128]{2,1,0:T(8,128)(2,1)S(1)}, s16[48,16,128]{2,1,...) custom-call(s32[64]{0:T(128)} %bitcast.15, ...), custom_call_target="tpu_custom_call" | custom-call | tf_op jit(solution)/shard_map/pallas_call | solution.py:113
  5.3 3.1 %collective-permute-start.1 = (s16[48,16,128]{2,1,0:T(8,128)(2,1)S(1)}, s16[48,16,128]{2,1,0:T(8,128)(2,1)S(1)}, u32[]{:S(2)}, u32[]{:S(2)}) collective-permute-start(s16[48,16,128]{2,1,0:T(8,128)(2,1)S(1)} %get-tuple-element.13), channel_id=1, source_target_pairs={{0,8},{1,9},{2,10},{3,11},{4,12},{5,13},{6,14},{7,15},{8,0},{9,1},... | collective-permute-start | bytes 589832 | tf_op jit(solution)/shard_map/ppermute | solution.py:215
  8.4 0.0 copy-done
  8.4 0.0 collective-permute-start
  8.4 1.5 %collective-permute-start.5 = (s16[48,16,128]{2,1,0:T(8,128)(2,1)S(1)}, s16[48,16,128]{2,1,0:T(8,128)(2,1)S(1)}, u32[]{:S(2)}, u32[]{:S(2)}) collective-permute-start(s16[48,16,128]{2,1,0:T(8,128)(2,1)S(1)} %get-tuple-element.15), channel_id=1, source_target_pairs={{0,2},{1,5},{2,0},{3,7},{4,6},{5,1},{6,4},{7,3},{8,10},{9,13},{10,... | collective-permute-start | bytes 589832 | tf_op jit(solution)/shard_map/ppermute | solution.py:215
  9.9 1.5 %collective-permute-start.9 = (s16[48,16,128]{2,1,0:T(8,128)(2,1)S(1)}, s16[48,16,128]{2,1,0:T(8,128)(2,1)S(1)}, u32[]{:S(2)}, u32[]{:S(2)}) collective-permute-start(s16[48,16,128]{2,1,0:T(8,128)(2,1)S(1)} %get-tuple-element.17), channel_id=1, source_target_pairs={{0,4},{1,3},{2,6},{3,1},{4,0},{5,7},{6,2},{7,5},{8,12},{9,11},{10,... | collective-permute-start | bytes 589832 | tf_op jit(solution)/shard_map/ppermute | solution.py:215
  11.4 0.5 %collective-permute-start.13 = (s16[48,16,128]{2,1,0:T(8,128)(2,1)S(1)}, s16[48,16,128]{2,1,0:T(8,128)(2,1)S(1)}, u32[]{:S(2)}, u32[]{:S(2)}) collective-permute-start(s16[48,16,128]{2,1,0:T(8,128)(2,1)S(1)} %get-tuple-element.19), channel_id=1, source_target_pairs={{0,4},{1,3},{2,6},{3,1},{4,0},{5,7},{6,2},{7,5},{8,12},{9,11},{10,... | collective-permute-start | bytes 589832 | tf_op jit(solution)/shard_map/ppermute | solution.py:215
  11.9 1.4 %collective-permute-done.1.refs_1_ = s16[48,16,128]{2,1,0:T(8,128)(2,1)S(1)} collective-permute-done((s16[48,16,128]{2,1,0:T(8,128)(2,1)S(1)}, s16[48,16,128]{2,1,0:T(8,128)(2,1)S(1)}, u32[]{:S(2)}, u32[]{:S(2)}) %collective-permute-start.1) | collective-permute-done | bytes 196640 | tf_op jit(solution)/shard_map/ppermute | solution.py:215
  13.3 0.1 minimum_convert_fusion.3
  13.4 2.8 %collective-permute-start.2 = (s16[24,16,128]{2,1,0:T(8,128)(2,1)S(1)}, s16[24,16,128]{2,1,0:T(8,128)(2,1)S(1)}, u32[]{:S(2)}, u32[]{:S(2)}) collective-permute-start(s16[24,16,128]{2,1,0:T(8,128)(2,1)S(1)} %minimum_convert_fusion.3), channel_id=1, source_target_pairs={{0,16},{1,17},{2,18},{3,19},{4,20},{5,21},{6,22},{7,23},{8,24},{9,... | collective-permute-start | bytes 294920 | tf_op jit(solution)/shard_map/ppermute | solution.py:215
  16.2 0.0 collective-permute-done.5.refs_6_
  16.2 0.1 minimum_convert_fusion.2
  16.3 1.6 %collective-permute-start.6 = (s16[24,16,128]{2,1,0:T(8,128)(2,1)S(1)}, s16[24,16,128]{2,1,0:T(8,128)(2,1)S(1)}, u32[]{:S(2)}, u32[]{:S(2)}) collective-permute-start(s16[24,16,128]{2,1,0:T(8,128)(2,1)S(1)} %minimum_convert_fusion.2), channel_id=1, source_target_pairs={{0,4},{1,3},{2,6},{3,1},{4,0},{5,7},{6,2},{7,5},{8,12},{9,11},{10,... | collective-permute-start | bytes 294920 | tf_op jit(solution)/shard_map/ppermute | solution.py:215
  17.8 0.0 collective-permute-done.9.refs_11_
  17.8 0.1 minimum_convert_fusion.1
  17.9 1.6 %collective-permute-start.10 = (s16[24,16,128]{2,1,0:T(8,128)(2,1)S(1)}, s16[24,16,128]{2,1,0:T(8,128)(2,1)S(1)}, u32[]{:S(2)}, u32[]{:S(2)}) collective-permute-start(s16[24,16,128]{2,1,0:T(8,128)(2,1)S(1)} %minimum_convert_fusion.1), channel_id=1, source_target_pairs={{0,2},{1,5},{2,0},{3,7},{4,6},{5,1},{6,4},{7,3},{8,10},{9,13},{10,... | collective-permute-start | bytes 294920 | tf_op jit(solution)/shard_map/ppermute | solution.py:215
  19.5 0.0 collective-permute-done.13.refs_16_
  19.5 0.1 minimum_convert_fusion
  19.6 0.6 %collective-permute-start.14 = (s16[24,16,128]{2,1,0:T(8,128)(2,1)S(1)}, s16[24,16,128]{2,1,0:T(8,128)(2,1)S(1)}, u32[]{:S(2)}, u32[]{:S(2)}) collective-permute-start(s16[24,16,128]{2,1,0:T(8,128)(2,1)S(1)} %minimum_convert_fusion), channel_id=1, source_target_pairs={{0,2},{1,5},{2,0},{3,7},{4,6},{5,1},{6,4},{7,3},{8,10},{9,13},{10,... | collective-permute-start | bytes 294920 | tf_op jit(solution)/shard_map/ppermute | solution.py:215
  20.2 0.3 collective-permute-done.2.refs_2_
  20.4 0.1 minimum_convert_fusion.7
  20.5 1.4 %collective-permute-start.3 = (s16[12,16,128]{2,1,0:T(8,128)(2,1)S(1)}, s16[12,16,128]{2,1,0:T(8,128)(2,1)S(1)}, u32[]{:S(2)}, u32[]{:S(2)}) collective-permute-start(s16[12,16,128]{2,1,0:T(8,128)(2,1)S(1)} %minimum_convert_fusion.7), channel_id=1, source_target_pairs={{0,2},{1,5},{2,0},{3,7},{4,6},{5,1},{6,4},{7,3},{8,10},{9,13},{10,... | collective-permute-start | bytes 147464 | tf_op jit(solution)/shard_map/ppermute | solution.py:215
  21.9 0.0 collective-permute-done.6.refs_7_
  21.9 0.1 minimum_convert_fusion.6
  21.9 1.6 %collective-permute-start.7 = (s16[12,16,128]{2,1,0:T(8,128)(2,1)S(1)}, s16[12,16,128]{2,1,0:T(8,128)(2,1)S(1)}, u32[]{:S(2)}, u32[]{:S(2)}) collective-permute-start(s16[12,16,128]{2,1,0:T(8,128)(2,1)S(1)} %minimum_convert_fusion.6), channel_id=1, source_target_pairs={{0,8},{1,9},{2,10},{3,11},{4,12},{5,13},{6,14},{7,15},{8,0},{9,1},... | collective-permute-start | bytes 147464 | tf_op jit(solution)/shard_map/ppermute | solution.py:215
  23.5 0.0 collective-permute-done.10.refs_12_
  23.5 0.1 minimum_convert_fusion.5
  23.6 0.8 %collective-permute-start.11 = (s16[12,16,128]{2,1,0:T(8,128)(2,1)S(1)}, s16[12,16,128]{2,1,0:T(8,128)(2,1)S(1)}, u32[]{:S(2)}, u32[]{:S(2)}) collective-permute-start(s16[12,16,128]{2,1,0:T(8,128)(2,1)S(1)} %minimum_convert_fusion.5), channel_id=1, source_target_pairs={{0,8},{1,9},{2,10},{3,11},{4,12},{5,13},{6,14},{7,15},{8,0},{9,1},... | collective-permute-start | bytes 147464 | tf_op jit(solution)/shard_map/ppermute | solution.py:215
  24.3 0.0 collective-permute-done.14.refs_17_
  24.3 0.1 minimum_convert_fusion.4
  24.4 1.6 %collective-permute-start.15 = (s16[12,16,128]{2,1,0:T(8,128)(2,1)S(1)}, s16[12,16,128]{2,1,0:T(8,128)(2,1)S(1)}, u32[]{:S(2)}, u32[]{:S(2)}) collective-permute-start(s16[12,16,128]{2,1,0:T(8,128)(2,1)S(1)} %minimum_convert_fusion.4), channel_id=1, source_target_pairs={{0,8},{1,9},{2,10},{3,11},{4,12},{5,13},{6,14},{7,15},{8,0},{9,1},... | collective-permute-start | bytes 147464 | tf_op jit(solution)/shard_map/ppermute | solution.py:215
  26.0 0.0 collective-permute-done.3.refs_3_
  26.0 1.6 %collective-permute-start.4 = (s16[6,16,128]{2,1,0:T(8,128)(2,1)S(1)}, s16[6,16,128]{2,1,0:T(8,128)(2,1)S(1)}, u32[]{:S(2)}, u32[]{:S(2)}) collective-permute-start(s16[6,16,128]{2,1,0:T(8,128)(2,1)S(1)} %minimum_convert_fusion.11), channel_id=1, source_target_pairs={{0,4},{1,3},{2,6},{3,1},{4,0},{5,7},{6,2},{7,5},{8,12},{9,11},{10,... | collective-permute-start | bytes 73736 | tf_op jit(solution)/shard_map/ppermute | solution.py:215
  27.6 0.0 collective-permute-done.7.refs_8_
  27.6 2.5 %collective-permute-start.8 = (s16[6,16,128]{2,1,0:T(8,128)(2,1)S(1)}, s16[6,16,128]{2,1,0:T(8,128)(2,1)S(1)}, u32[]{:S(2)}, u32[]{:S(2)}) collective-permute-start(s16[6,16,128]{2,1,0:T(8,128)(2,1)S(1)} %minimum_convert_fusion.10), channel_id=1, source_target_pairs={{0,16},{1,17},{2,18},{3,19},{4,20},{5,21},{6,22},{7,23},{8,24},{9,... | collective-permute-start | bytes 73736 | tf_op jit(solution)/shard_map/ppermute | solution.py:215
  30.1 0.0 collective-permute-done.11.refs_13_
  30.1 0.0 copy-start.3
  30.1 0.6 %collective-permute-start.12 = (s16[6,16,128]{2,1,0:T(8,128)(2,1)S(1)}, s16[6,16,128]{2,1,0:T(8,128)(2,1)S(1)}, u32[]{:S(2)}, u32[]{:S(2)}) collective-permute-start(s16[6,16,128]{2,1,0:T(8,128)(2,1)S(1)} %minimum_convert_fusion.9), channel_id=1, source_target_pairs={{0,16},{1,17},{2,18},{3,19},{4,20},{5,21},{6,22},{7,23},{8,24},{9,... | collective-permute-start | bytes 73736 | tf_op jit(solution)/shard_map/ppermute | solution.py:215
  30.7 0.0 collective-permute-done.15.refs_18_
  30.8 0.0 copy-start.1
  30.8 0.0 copy-start.2
  30.8 2.5 %collective-permute-start.16 = (s16[6,16,128]{2,1,0:T(8,128)(2,1)S(1)}, s16[6,16,128]{2,1,0:T(8,128)(2,1)S(1)}, u32[]{:S(2)}, u32[]{:S(2)}) collective-permute-start(s16[6,16,128]{2,1,0:T(8,128)(2,1)S(1)} %minimum_convert_fusion.8), channel_id=1, source_target_pairs={{0,16},{1,17},{2,18},{3,19},{4,20},{5,21},{6,22},{7,23},{8,24},{9,... | collective-permute-start | bytes 73736 | tf_op jit(solution)/shard_map/ppermute | solution.py:215
  33.3 0.0 copy-done.3
  33.3 0.1 copy.15.rblock_ref
  33.4 0.0 collective-permute-done.other_ref
  33.4 0.0 collective-permute-done.4.refs_4_
  33.4 0.0 collective-permute-done.8.refs_9_
  33.4 1.6 %collective-permute-done.12.refs_14_ = s16[6,16,128]{2,1,0:T(8,128)(2,1)S(1)} collective-permute-done((s16[6,16,128]{2,1,0:T(8,128)(2,1)S(1)}, s16[6,16,128]{2,1,0:T(8,128)(2,1)S(1)}, u32[]{:S(2)}, u32[]{:S(2)}) %collective-permute-start.12) | collective-permute-done | bytes 24608 | tf_op jit(solution)/shard_map/ppermute | solution.py:215
  34.9 0.7 %collective-permute-done.16.refs_19_ = s16[6,16,128]{2,1,0:T(8,128)(2,1)S(1)} collective-permute-done((s16[6,16,128]{2,1,0:T(8,128)(2,1)S(1)}, s16[6,16,128]{2,1,0:T(8,128)(2,1)S(1)}, u32[]{:S(2)}, u32[]{:S(2)}) %collective-permute-start.16) | collective-permute-done | bytes 24608 | tf_op jit(solution)/shard_map/ppermute | solution.py:215
  35.6 0.0 copy-done.1
  35.6 0.0 copy-done.2
  35.6 1.5 %shard_map.141 = (f32[64,768]{1,0:T(8,128)}, f32[16,16,128]{2,1,0:T(8,128)S(1)}) custom-call(s32[6,2]{1,0:T(8,128)S(1)} %copy.15.rblock_ref, f32[6,128]{1,0:T(8,128)S(1)} %bitcast.9, f32[6,128]{1,0:T(8,128)S(1)} %bitcast.10, bf16[6,2,64,128]{3,2,1,0:T(8,128)(2,1)S(1)} %copy-done, bf16[6,2,64,128]{3,2,1,0:T(8,128)(2,1)S(1)} %collective-permute-done.other_ref, ...), custom_call_target="tpu_custom_call" | custom-call | tf_op jit(solution)/shard_map/pallas_call | solution.py:169
  37.1 11.9 %all_to_all.5 = f32[16,16,128]{2,1,0:T(8,128)S(1)} all-to-all(f32[16,16,128]{2,1,0:T(8,128)S(1)} %get-tuple-element.21), channel_id=1, replica_groups=mesh['risk'=16,'tcol'=2] {'risk'}, dimensions={0} | all-to-all | bytes 262144 | tf_op jit(solution)/shard_map/all_to_all | solution.py:222
  49.0 0.1 slice_reduce_fusion.1
  49.1 0.6 %maximum_bitcast_fusion = f32[64,32]{0,1:T(8,128)} fusion(f32[16,64]{1,0:T(8,128)S(1)} %get-tuple-element.23, f32[16,64]{1,0:T(8,128)S(1)} %get-tuple-element.22), kind=kLoop, calls=%fused_computation.14 | loop fusion | flops 2048 | bytes 16384 | tf_op jit(solution)/shard_map/transpose | solution.py:184
  (4 shorter events, 0.1 us)
Async XLA Ops:
  0.6 7.8 %copy-start = (bf16[6,2,64,128]{3,2,1,0:T(8,128)(2,1)S(1)}, bf16[6,2,64,128]{3,2,1,0:T(8,128)(2,1)}, u32[]{:S(2)}) copy-start(bf16[6,2,64,128]{3,2,1,0:T(8,128)(2,1)} %mine_ref.1) | copy-start | bytes 589828
  5.3 8.0 %collective-permute-start.1 = (s16[48,16,128]{2,1,0:T(8,128)(2,1)S(1)}, s16[48,16,128]{2,1,0:T(8,128)(2,1)S(1)}, u32[]{:S(2)}, u32[]{:S(2)}) collective-permute-start(s16[48,16,128]{2,1,0:T(8,128)(2,1)S(1)} %get-tuple-element.13), channel_id=1, source_target_pairs={{0,8},{1,9},{2,10},{3,11},{4,12},{5,13},{6,14},{7,15},{8,0},{9,1},... | collective-permute-start | bytes 589832 | tf_op jit(solution)/shard_map/ppermute | solution.py:215
  8.4 25.0 %collective-permute-start = (bf16[6,2,64,128]{3,2,1,0:T(8,128)(2,1)S(1)}, bf16[6,2,64,128]{3,2,1,0:T(8,128)(2,1)S(1)}, u32[]{:S(2)}, u32[]{:S(2)}) collective-permute-start(bf16[6,2,64,128]{3,2,1,0:T(8,128)(2,1)S(1)} %copy-done), channel_id=1, source_target_pairs={{0,1},{1,0},{2,3},{3,2},{4,5},{5,4},{6,7},{7,6},{8,9},{9,8},{10,11... | collective-permute-start | bytes 589832 | tf_op jit(solution)/shard_map/ppermute | solution.py:201
  8.4 7.8 %collective-permute-start.5 = (s16[48,16,128]{2,1,0:T(8,128)(2,1)S(1)}, s16[48,16,128]{2,1,0:T(8,128)(2,1)S(1)}, u32[]{:S(2)}, u32[]{:S(2)}) collective-permute-start(s16[48,16,128]{2,1,0:T(8,128)(2,1)S(1)} %get-tuple-element.15), channel_id=1, source_target_pairs={{0,2},{1,5},{2,0},{3,7},{4,6},{5,1},{6,4},{7,3},{8,10},{9,13},{10,... | collective-permute-start | bytes 589832 | tf_op jit(solution)/shard_map/ppermute | solution.py:215
  9.9 8.0 %collective-permute-start.9 = (s16[48,16,128]{2,1,0:T(8,128)(2,1)S(1)}, s16[48,16,128]{2,1,0:T(8,128)(2,1)S(1)}, u32[]{:S(2)}, u32[]{:S(2)}) collective-permute-start(s16[48,16,128]{2,1,0:T(8,128)(2,1)S(1)} %get-tuple-element.17), channel_id=1, source_target_pairs={{0,4},{1,3},{2,6},{3,1},{4,0},{5,7},{6,2},{7,5},{8,12},{9,11},{10,... | collective-permute-start | bytes 589832 | tf_op jit(solution)/shard_map/ppermute | solution.py:215
  11.4 8.1 %collective-permute-start.13 = (s16[48,16,128]{2,1,0:T(8,128)(2,1)S(1)}, s16[48,16,128]{2,1,0:T(8,128)(2,1)S(1)}, u32[]{:S(2)}, u32[]{:S(2)}) collective-permute-start(s16[48,16,128]{2,1,0:T(8,128)(2,1)S(1)} %get-tuple-element.19), channel_id=1, source_target_pairs={{0,4},{1,3},{2,6},{3,1},{4,0},{5,7},{6,2},{7,5},{8,12},{9,11},{10,... | collective-permute-start | bytes 589832 | tf_op jit(solution)/shard_map/ppermute | solution.py:215
  13.4 7.0 %collective-permute-start.2 = (s16[24,16,128]{2,1,0:T(8,128)(2,1)S(1)}, s16[24,16,128]{2,1,0:T(8,128)(2,1)S(1)}, u32[]{:S(2)}, u32[]{:S(2)}) collective-permute-start(s16[24,16,128]{2,1,0:T(8,128)(2,1)S(1)} %minimum_convert_fusion.3), channel_id=1, source_target_pairs={{0,16},{1,17},{2,18},{3,19},{4,20},{5,21},{6,22},{7,23},{8,24},{9,... | collective-permute-start | bytes 294920 | tf_op jit(solution)/shard_map/ppermute | solution.py:215
  16.3 5.6 %collective-permute-start.6 = (s16[24,16,128]{2,1,0:T(8,128)(2,1)S(1)}, s16[24,16,128]{2,1,0:T(8,128)(2,1)S(1)}, u32[]{:S(2)}, u32[]{:S(2)}) collective-permute-start(s16[24,16,128]{2,1,0:T(8,128)(2,1)S(1)} %minimum_convert_fusion.2), channel_id=1, source_target_pairs={{0,4},{1,3},{2,6},{3,1},{4,0},{5,7},{6,2},{7,5},{8,12},{9,11},{10,... | collective-permute-start | bytes 294920 | tf_op jit(solution)/shard_map/ppermute | solution.py:215
  17.9 5.6 %collective-permute-start.10 = (s16[24,16,128]{2,1,0:T(8,128)(2,1)S(1)}, s16[24,16,128]{2,1,0:T(8,128)(2,1)S(1)}, u32[]{:S(2)}, u32[]{:S(2)}) collective-permute-start(s16[24,16,128]{2,1,0:T(8,128)(2,1)S(1)} %minimum_convert_fusion.1), channel_id=1, source_target_pairs={{0,2},{1,5},{2,0},{3,7},{4,6},{5,1},{6,4},{7,3},{8,10},{9,13},{10,... | collective-permute-start | bytes 294920 | tf_op jit(solution)/shard_map/ppermute | solution.py:215
  19.6 4.7 %collective-permute-start.14 = (s16[24,16,128]{2,1,0:T(8,128)(2,1)S(1)}, s16[24,16,128]{2,1,0:T(8,128)(2,1)S(1)}, u32[]{:S(2)}, u32[]{:S(2)}) collective-permute-start(s16[24,16,128]{2,1,0:T(8,128)(2,1)S(1)} %minimum_convert_fusion), channel_id=1, source_target_pairs={{0,2},{1,5},{2,0},{3,7},{4,6},{5,1},{6,4},{7,3},{8,10},{9,13},{10,... | collective-permute-start | bytes 294920 | tf_op jit(solution)/shard_map/ppermute | solution.py:215
  20.5 5.5 %collective-permute-start.3 = (s16[12,16,128]{2,1,0:T(8,128)(2,1)S(1)}, s16[12,16,128]{2,1,0:T(8,128)(2,1)S(1)}, u32[]{:S(2)}, u32[]{:S(2)}) collective-permute-start(s16[12,16,128]{2,1,0:T(8,128)(2,1)S(1)} %minimum_convert_fusion.7), channel_id=1, source_target_pairs={{0,2},{1,5},{2,0},{3,7},{4,6},{5,1},{6,4},{7,3},{8,10},{9,13},{10,... | collective-permute-start | bytes 147464 | tf_op jit(solution)/shard_map/ppermute | solution.py:215
  21.9 5.7 %collective-permute-start.7 = (s16[12,16,128]{2,1,0:T(8,128)(2,1)S(1)}, s16[12,16,128]{2,1,0:T(8,128)(2,1)S(1)}, u32[]{:S(2)}, u32[]{:S(2)}) collective-permute-start(s16[12,16,128]{2,1,0:T(8,128)(2,1)S(1)} %minimum_convert_fusion.6), channel_id=1, source_target_pairs={{0,8},{1,9},{2,10},{3,11},{4,12},{5,13},{6,14},{7,15},{8,0},{9,1},... | collective-permute-start | bytes 147464 | tf_op jit(solution)/shard_map/ppermute | solution.py:215
  23.6 6.5 %collective-permute-start.11 = (s16[12,16,128]{2,1,0:T(8,128)(2,1)S(1)}, s16[12,16,128]{2,1,0:T(8,128)(2,1)S(1)}, u32[]{:S(2)}, u32[]{:S(2)}) collective-permute-start(s16[12,16,128]{2,1,0:T(8,128)(2,1)S(1)} %minimum_convert_fusion.5), channel_id=1, source_target_pairs={{0,8},{1,9},{2,10},{3,11},{4,12},{5,13},{6,14},{7,15},{8,0},{9,1},... | collective-permute-start | bytes 147464 | tf_op jit(solution)/shard_map/ppermute | solution.py:215
  24.4 6.4 %collective-permute-start.15 = (s16[12,16,128]{2,1,0:T(8,128)(2,1)S(1)}, s16[12,16,128]{2,1,0:T(8,128)(2,1)S(1)}, u32[]{:S(2)}, u32[]{:S(2)}) collective-permute-start(s16[12,16,128]{2,1,0:T(8,128)(2,1)S(1)} %minimum_convert_fusion.4), channel_id=1, source_target_pairs={{0,8},{1,9},{2,10},{3,11},{4,12},{5,13},{6,14},{7,15},{8,0},{9,1},... | collective-permute-start | bytes 147464 | tf_op jit(solution)/shard_map/ppermute | solution.py:215
  26.0 7.4 %collective-permute-start.4 = (s16[6,16,128]{2,1,0:T(8,128)(2,1)S(1)}, s16[6,16,128]{2,1,0:T(8,128)(2,1)S(1)}, u32[]{:S(2)}, u32[]{:S(2)}) collective-permute-start(s16[6,16,128]{2,1,0:T(8,128)(2,1)S(1)} %minimum_convert_fusion.11), channel_id=1, source_target_pairs={{0,4},{1,3},{2,6},{3,1},{4,0},{5,7},{6,2},{7,5},{8,12},{9,11},{10,... | collective-permute-start | bytes 73736 | tf_op jit(solution)/shard_map/ppermute | solution.py:215
  27.6 5.7 %collective-permute-start.8 = (s16[6,16,128]{2,1,0:T(8,128)(2,1)S(1)}, s16[6,16,128]{2,1,0:T(8,128)(2,1)S(1)}, u32[]{:S(2)}, u32[]{:S(2)}) collective-permute-start(s16[6,16,128]{2,1,0:T(8,128)(2,1)S(1)} %minimum_convert_fusion.10), channel_id=1, source_target_pairs={{0,16},{1,17},{2,18},{3,19},{4,20},{5,21},{6,22},{7,23},{8,24},{9,... | collective-permute-start | bytes 73736 | tf_op jit(solution)/shard_map/ppermute | solution.py:215
  30.1 3.1 %copy-start.3 = (s32[6,2]{0,1:T(2,128)S(1)}, s32[6,2]{0,1:T(2,128)}, u32[]{:S(2)}) copy-start(s32[6,2]{0,1:T(2,128)} %param.25) | copy-start | bytes 148
  30.1 4.8 %collective-permute-start.12 = (s16[6,16,128]{2,1,0:T(8,128)(2,1)S(1)}, s16[6,16,128]{2,1,0:T(8,128)(2,1)S(1)}, u32[]{:S(2)}, u32[]{:S(2)}) collective-permute-start(s16[6,16,128]{2,1,0:T(8,128)(2,1)S(1)} %minimum_convert_fusion.9), channel_id=1, source_target_pairs={{0,16},{1,17},{2,18},{3,19},{4,20},{5,21},{6,22},{7,23},{8,24},{9,... | collective-permute-start | bytes 73736 | tf_op jit(solution)/shard_map/ppermute | solution.py:215
  30.8 4.9 %copy-start.1 = (f32[768]{0:T(1024)S(1)}, f32[768]{0:T(1024)}, u32[]{:S(2)}) copy-start(f32[768]{0:T(1024)} %param.22) | copy-start | bytes 9220
  30.8 4.8 %copy-start.2 = (f32[768]{0:T(1024)S(1)}, f32[768]{0:T(1024)}, u32[]{:S(2)}) copy-start(f32[768]{0:T(1024)} %param.23) | copy-start | bytes 9220
  30.8 4.8 %collective-permute-start.16 = (s16[6,16,128]{2,1,0:T(8,128)(2,1)S(1)}, s16[6,16,128]{2,1,0:T(8,128)(2,1)S(1)}, u32[]{:S(2)}, u32[]{:S(2)}) collective-permute-start(s16[6,16,128]{2,1,0:T(8,128)(2,1)S(1)} %minimum_convert_fusion.8), channel_id=1, source_target_pairs={{0,16},{1,17},{2,18},{3,19},{4,20},{5,21},{6,22},{7,23},{8,24},{9,... | collective-permute-start | bytes 73736 | tf_op jit(solution)/shard_map/ppermute | solution.py:215
